TPU v7x, 512 devices: a whole 4x8x8 slice. The times are simulated.
512 devices in a mesh: dp: 4 (over x), tm: 128 (over y, z, core).
Axes of the slice: x: 4, y: 8, z: 8, core: 2. Of those that a mesh axis runs over, the one named last changes fastest.
Arguments:
- query_rows: bfloat16 [4, 16384, 512], P('dp', 'tm'), may hold values from -60 to 60
- key_rows: bfloat16 [4, 16384, 512], P('dp', 'tm'), may hold values from -4 to 4
- value_rows: bfloat16 [4, 16384, 512], P('dp', 'tm'), may hold values from -6 to 6
- out_grad: bfloat16 [4, 16384, 1024], P('dp', 'tm'), may hold values from -6 to 6
- out_weight: bfloat16 [512, 1024], replicated, may hold values from -0.25 to 0.25
- memory_index: int32 [4, 128, 8], P('dp', 'tm'), may hold values from 0 to 127, as said below
Outputs:
- query_grad: bfloat16 [4, 16384, 512], P('dp', 'tm')
- key_grad: bfloat16 [4, 16384, 512], P('dp', 'tm')
- value_grad: bfloat16 [4, 16384, 512], P('dp', 'tm')
- weight_grad: bfloat16 [512, 1024], replicated
Inputs may be any that keep to these rules, and one draw needn't show every extreme that they name: `memory_index`: each row holds 8 distinct positions of its segment.
All inputs are finite; a program needn't handle non-finite values.
Results may differ from a plain program's by a relative error of at most 0.028.
Values may be sent and summed in bfloat16 or wider, within the bound.
A program may use at most 64 MiB of HBM per device.

v0:
```python
import math

import jax
import jax.numpy as jnp
from jax import lax
from jax.sharding import PartitionSpec as P

HEADS = 8
HEAD_DIM = 64


def split_heads(matrix):
    return matrix.reshape(matrix.shape[0], HEADS, HEAD_DIM).transpose(1, 0, 2)


def merge_heads(stacked):
    return stacked.transpose(1, 0, 2).reshape(stacked.shape[1], HEADS * HEAD_DIM)


def head_pass(query_head, key_head, value_head, mem_keys, mem_values, grad_head, alive_slots):
    inv_root = 1.0 / math.sqrt(HEAD_DIM)
    keys_all = jnp.concatenate([key_head, mem_keys], 0)
    values_all = jnp.concatenate([value_head, mem_values], 0)
    scores = jnp.dot(query_head, keys_all.T, preferred_element_type=jnp.float32) * inv_root
    mask_all = jnp.concatenate([jnp.ones((key_head.shape[0],), bool), alive_slots])
    scores = jnp.where(mask_all[None, :], scores, -jnp.inf)
    row_max = jnp.max(scores, axis=1, keepdims=True)
    exp_scores = jnp.exp(scores - row_max)
    soft_weights = exp_scores / jnp.sum(exp_scores, axis=1, keepdims=True)
    soft_low = soft_weights.astype(jnp.bfloat16)
    attended = jnp.dot(soft_low, values_all, preferred_element_type=jnp.float32).astype(
        jnp.bfloat16
    )
    row_delta = jnp.sum(
        grad_head.astype(jnp.float32) * attended.astype(jnp.float32), axis=1, keepdims=True
    )
    grad_soft = jnp.dot(grad_head, values_all.T, preferred_element_type=jnp.float32)
    grad_score = (soft_weights * (grad_soft - row_delta)).astype(jnp.bfloat16)
    grad_query = (
        jnp.dot(grad_score, keys_all, preferred_element_type=jnp.float32) * inv_root
    ).astype(jnp.bfloat16)
    grad_keys = jnp.dot(grad_score.T, query_head, preferred_element_type=jnp.float32) * inv_root
    grad_values = jnp.dot(soft_low.T, grad_head, preferred_element_type=jnp.float32)
    return (attended, grad_query, grad_keys, grad_values)


def on_device(query_rows, key_rows, value_rows, out_grad, out_weight, memory_index):
    segment = lax.axis_index("tm")
    count_seg = lax.axis_size("tm")
    query_seg = query_rows[0]
    key_seg = key_rows[0]
    value_seg = value_rows[0]
    grad_seg = out_grad[0]
    picked = memory_index[0, 0]
    seg_len = query_seg.shape[0]
    memory = picked.shape[0]
    own_keys = jnp.take(key_seg, picked, axis=0)
    own_values = jnp.take(value_seg, picked, axis=0)
    mem_keys, mem_values = (
        lax.all_gather(own_keys, "tm", axis=0, tiled=True),
        lax.all_gather(own_values, "tm", axis=0, tiled=True),
    )
    mem_slots = mem_keys.shape[0]
    alive_slots = jnp.arange(mem_slots, dtype=jnp.int32) // memory < segment
    grad_attn = lax.dot_general(
        grad_seg, out_weight, (((1,), (1,)), ((), ())), preferred_element_type=jnp.float32
    ).astype(jnp.bfloat16)

    def per_head(packed):
        return head_pass(
            packed[0], packed[1], packed[2], packed[3], packed[4], packed[5], alive_slots
        )

    attended, grad_query, grad_keys, grad_values = lax.map(
        per_head,
        (
            split_heads(query_seg),
            split_heads(key_seg),
            split_heads(value_seg),
            split_heads(mem_keys),
            split_heads(mem_values),
            split_heads(grad_attn),
        ),
    )
    attended_rows = merge_heads(attended)
    key_all = merge_heads(grad_keys)
    value_all = merge_heads(grad_values)
    local_key = key_all[:seg_len]
    local_value = value_all[:seg_len]
    slot_keys = key_all[seg_len:]
    slot_values = value_all[seg_len:]
    own_key_grad, own_value_grad = (
        lax.psum_scatter(slot_keys, "tm", scatter_dimension=0, tiled=True),
        lax.psum_scatter(slot_values, "tm", scatter_dimension=0, tiled=True),
    )
    key_grad = local_key.at[picked].add(own_key_grad).astype(jnp.bfloat16)
    value_grad = local_value.at[picked].add(own_value_grad).astype(jnp.bfloat16)
    weight_term = lax.dot_general(
        attended_rows, grad_seg, (((0,), (0,)), ((), ())), preferred_element_type=jnp.float32
    )
    grad_norm = 1.0 / math.sqrt(lax.axis_size("dp") * count_seg * seg_len)
    summed = lax.psum(weight_term, ("dp", "tm"))
    weight_grad = (summed * grad_norm).astype(jnp.bfloat16)
    return (merge_heads(grad_query)[None], key_grad[None], value_grad[None], weight_grad)


def solution(mesh):
    placed = (
        P("dp", "tm", None),
        P("dp", "tm", None),
        P("dp", "tm", None),
        P("dp", "tm", None),
        P(),
        P("dp", "tm", None),
    )
    return jax.shard_map(
        on_device,
        mesh=mesh,
        in_specs=placed,
        out_specs=(P("dp", "tm", None), P("dp", "tm", None), P("dp", "tm", None), P()),
        check_vma=False,
    )
```

profile of v0, /device:TPU:1, one launch (start us, length us, event | category | flops | bytes accessed | tf_op | source)
XLA Modules:
  0.0 933.4 jit_solution(15962856685089660133)
XLA Ops:
  8.6 1.5 gather_fusion
  10.1 1.5 gather_fusion.1
  13.2 1.7 copy.49
  14.8 1.7 copy.51
  16.5 1.4 convolution_convert_fusion.1
  18.8 78.8 %all-gather.5.cloned.1.call-done = bf16[1024,512]{1,0:T(8,128)(2,1)} async-done(((bf16[8,512]{1,0:T(8,128)(2,1)}), bf16[1024,512]{1,0:T(8,128)(2,1)}) %all-gather.5.cloned.1.call-update) | async-done | bytes 1048592 | tf_op jit(solution)/shard_map/all_gather | solution.py:61
  97.7 1.5 copy.52
  99.1 76.5 %all-gather.3.cloned.1.call-done = bf16[1024,512]{1,0:T(8,128)(2,1)} async-done(((bf16[8,512]{1,0:T(8,128)(2,1)}), bf16[1024,512]{1,0:T(8,128)(2,1)}) %all-gather.3.cloned.1.call-update) | async-done | bytes 1048592 | tf_op jit(solution)/shard_map/all_gather | solution.py:60
  175.6 2.3 copy.50
  177.9 73.1 %while.17 = (s32[]{:T(128)}, bf16[8,128,64]{1,2,0:T(8,128)(2,1)}, bf16[8,128,64]{1,2,0:T(8,128)(2,1)}, f32[8,1152,64]{1,2,0:T(8,128)}, f32[8,1152,64]{1,2,0:T(8,...) while((s32[]{:T(128)}, bf16[8,128,64]{1,2,0:T(8,128)(2,1)}, ...), condition=%wide.region_4.6_spmd.clone, body=%wide.region_0.5_spmd.clone.sunk | while | flops 116925056 | bytes 6502682 | solution.py:74
  177.9 0.9 constant_dynamic-slice_fusion.6
  180.5 1.7 fusion.71
  182.5 0.9 bitcast_dynamic-update-slice_fusion.2
  184.2 1.0 fusion.68
  186.1 0.9 fusion.69
  187.0 0.9 constant_dynamic-slice_fusion.6
  189.6 1.7 fusion.71
  191.7 0.9 bitcast_dynamic-update-slice_fusion.2
  193.3 1.0 fusion.68
  194.3 0.9 fusion.70
  195.2 0.9 fusion.69
  196.1 0.9 constant_dynamic-slice_fusion.6
  198.8 1.8 fusion.71
  200.8 0.9 bitcast_dynamic-update-slice_fusion.2
  202.5 1.0 fusion.68
  203.5 0.9 fusion.70
  205.3 0.9 constant_dynamic-slice_fusion.6
  207.9 1.7 fusion.71
  209.9 0.9 bitcast_dynamic-update-slice_fusion.2
  211.6 1.0 fusion.68
  214.4 0.9 constant_dynamic-slice_fusion.6
  217.0 1.8 fusion.71
  219.1 0.9 bitcast_dynamic-update-slice_fusion.2
  220.8 1.0 fusion.68
  221.8 0.9 fusion.70
  223.6 0.9 constant_dynamic-slice_fusion.6
  226.2 1.8 fusion.71
  228.2 0.9 bitcast_dynamic-update-slice_fusion.2
  229.9 1.0 fusion.68
  230.9 0.9 fusion.70
  232.7 0.9 constant_dynamic-slice_fusion.6
  235.3 1.7 fusion.71
  237.4 0.9 bitcast_dynamic-update-slice_fusion.2
  239.0 1.0 fusion.68
  240.0 0.9 fusion.70
  241.0 0.9 fusion.69
  241.9 0.9 constant_dynamic-slice_fusion.6
  244.5 1.7 fusion.71
  246.5 0.9 bitcast_dynamic-update-slice_fusion.2
  248.2 1.0 fusion.68
  249.2 0.9 fusion.70
  251.0 2.8 fusion.37
  253.9 1.7 slice.39
  255.6 1.9 copy.66
  257.6 1.7 slice.37
  259.3 1.9 copy.64
  261.3 1.0 slice.38
  262.3 1.0 slice.36
  264.3 264.4 %all-reduce.3.cloned.1.call-done = f32[512,1024]{1,0:T(8,128)} async-done(((f32[512,1024]{1,0:T(8,128)}), f32[512,1024]{1,0:T(8,128)}) %all-reduce.3.cloned.1.call-update) | async-done | bytes 2097168 | tf_op jit(solution)/shard_map/psum | solution.py:102
  528.7 2.8 multiply_convert_fusion
  531.5 192.7 %reduce-scatter.9.cloned.1.call-done = f32[8,512]{1,0:T(8,128)} async-done(((f32[1024,512]{1,0:T(8,128)}), f32[8,512]{1,0:T(8,128)}) %reduce-scatter.9.cloned.1.call-update) | async-done | bytes 16400 | tf_op jit(solution)/shard_map/reduce_scatter | solution.py:94
  724.2 0.9 scatter_fusion.1
  725.8 199.4 %reduce-scatter.7.cloned.1.call-done = f32[8,512]{1,0:T(8,128)} async-done(((f32[1024,512]{1,0:T(8,128)}), f32[8,512]{1,0:T(8,128)}) %reduce-scatter.7.cloned.1.call-update) | async-done | bytes 16400 | tf_op jit(solution)/shard_map/reduce_scatter | solution.py:93
  925.2 0.9 scatter_fusion
  (121 shorter events, 34.1 us)
Async XLA Ops:
  7.2 9.3 copy-start
  7.2 11.5 %copy-start.1 = (bf16[1,128,512]{2,1,0:T(8,128)(2,1)S(1)}, bf16[1,128,512]{2,1,0:T(8,128)(2,1)}, u32[]{:S(2)}) copy-start(bf16[1,128,512]{2,1,0:T(8,128)(2,1)} %param.10) | copy-start | bytes 393220
  7.2 90.5 %all-gather.5.cloned.1.call-start = ((), (), s32[]{:S(2)}) async-start(), calls=%async_computation.3 | async-start | bytes 1056768 | tf_op jit(solution)/shard_map/all_gather | solution.py:61
  12.3 163.3 %all-gather.3.cloned.1.call-start = ((), (), s32[]{:S(2)}) async-start(), calls=%async_computation.2 | async-start | bytes 1056768 | tf_op jit(solution)/shard_map/all_gather | solution.py:60
  13.1 515.6 %all-reduce.3.cloned.1.call-start = ((), (), s32[]{:S(2)}) async-start(), calls=%async_computation.4 | async-start | bytes 4194304 | tf_op jit(solution)/shard_map/psum | solution.py:102
  253.9 470.4 %reduce-scatter.9.cloned.1.call-start = ((), (), s32[]{:S(2)}) async-start(), calls=%async_computation.6 | async-start | bytes 2113536 | tf_op jit(solution)/shard_map/reduce_scatter | solution.py:94
  257.5 667.7 %reduce-scatter.7.cloned.1.call-start = ((), (), s32[]{:S(2)}) async-start(), calls=%async_computation.5 | async-start | bytes 2113536 | tf_op jit(solution)/shard_map/reduce_scatter | solution.py:93
  259.3 2.0 copy-start.3
  261.2 2.3 copy-start.2
Sparse Core Ops, SparseCore 0:
  12.5 85.1 all-gather.4
  100.7 74.8 all-gather.2
  254.0 274.7 all-reduce.2
  533.5 190.6 reduce-scatter.8
  729.0 196.1 reduce-scatter.6
where the time goes:
time: 941 us; the launch traced here: 933 us
  waiting for transfers between devices  813 us (86%)
  matrix products  51.1 us (5%)
  local copies, waits for them, and re-layouts  39.1 us (4%)
  other arithmetic  16.1 us (2%)
  between operations  13.9 us (1%)
    psum x1, waiting for transfers between devices, on_device(): summed = lax.psum(weight_term, ('dp', 'tm'))  264 us
    reduce_scatter x1, waiting for transfers between devices, on_device(): lax.psum_scatter(slot_keys, 'tm', scatter_dimension=0, tiled=True)  199 us
    reduce_scatter x1, waiting for transfers between devices, on_device(): lax.psum_scatter(slot_values, 'tm', scatter_dimension=0, tiled=True)  193 us
    all_gather x1, waiting for transfers between devices, on_device(): lax.all_gather(own_values, 'tm', axis=0, tiled=True)  78.8 us
    all_gather x1, waiting for transfers between devices, on_device(): lax.all_gather(own_keys, 'tm', axis=0, tiled=True)  76.5 us
  transfers between devices with their start and end apart: 5, of which 5 were waited for; matrix products, arithmetic and copies ran while one was open for 2% of the time, Pallas kernels for 0%

commit v1 on v0

v1 whole, which is shorter than its diff:
```python
import math

import jax
import jax.numpy as jnp
from jax import lax
from jax.experimental import pallas as pl
from jax.experimental.pallas import tpu as pltpu
from jax.sharding import PartitionSpec as P

HEAD_DIM = 64
SEG = 128
MEM = 8
HD = 512
D = 1024
HALF = 256
HEADS = 4
COLS = HEADS * 2 * SEG
NY, NZ, NX = 8, 8, 4
MESH = pl.DeviceIdType.MESH
F32, BF16 = jnp.float32, jnp.bfloat16

(C_IDX, C_K, C_V, C_Q, C_G, KZ, KY, VY, VZ, RKY, RKZ, RVZ, RVY, WX, WY, WZ, GZ, GY, GX, GC, O_Q, O_K, O_V) = range(23)


def nt(a, b):
    return lax.dot_general(a, b, (((1,), (1,)), ((), ())), preferred_element_type=F32)


def tn(a, b):
    return lax.dot_general(a, b, (((0,), (0,)), ((), ())), preferred_element_type=F32)


def nn(a, b):
    return jnp.dot(a, b, preferred_element_type=F32)


def rows8(block, op):
    return op(block.reshape(block.shape[0] // 8, 8, block.shape[1]), axis=0)


def kernel(
    idx_ref, q_ref, k_ref, v_ref, g_ref, w_ref,
    qo_ref, ko_ref, vo_ref, wo_ref,
    idxb, kp, vp, qp, gp, wh, q4, ga4, gat, oh, kbuf, vbuf, s_mem, s_loc,
    m8, l8, acc, qacc, kt, vt, kt_own, kg, vg, kry, krz, vrz, vry, ksum, vsum, vsum_own, krow, vrow,
    wt, wsend, wxr, wxs, wyr, wys, wzr, wg, obq, obk, obv,
    ssem, rsem, wsem,
):
    dp, tm = lax.axis_index("dp"), lax.axis_index("tm")
    c, z, y = tm % 2, (tm // 2) % NZ, tm // (2 * NZ)
    other = 1 - c

    def at_core():
        return (dp, y * 16 + z * 2 + other)

    def at_z(i):
        return (dp, y * 16 + i * 2 + c)

    def at_y(i):
        return (dp, i * 16 + z * 2 + c)

    def at_x(i):
        return (i, tm)

    def remote(src, dst, phase, mine, theirs, device):
        return pltpu.make_async_remote_copy(
            src_ref=src, dst_ref=dst, send_sem=ssem.at[phase, mine], recv_sem=rsem.at[phase, theirs],
            device_id=device, device_id_type=MESH,
        )

    def each(count, me, body):
        def step(d, _):
            body((me + d) % count)
            return 0

        lax.fori_loop(1, count, step, 0)

    def span(lo, hi, body):
        def step(i, _):
            body(i)
            return 0

        lax.fori_loop(lo, hi, step, 0)

    def blk(i):
        return pl.ds(pl.multiple_of(i * 16, 16), 16)

    my_cols = pl.ds(pl.multiple_of(c * HALF, HALF), HALF)
    their_cols = pl.ds(pl.multiple_of(other * HALF, HALF), HALF)

    vbuf[...] = jnp.zeros_like(vbuf)

    bar = pltpu.get_barrier_semaphore()

    def greet(device):
        pl.semaphore_signal(bar, inc=1, device_id=device, device_id_type=MESH)

    greet(at_core())
    each(NZ, z, lambda i: greet(at_z(i)))
    each(NY, y, lambda i: greet(at_y(i)))
    each(NX, dp, lambda i: greet(at_x(i)))

    w_copy = pltpu.make_async_copy(w_ref.at[pl.ds(pl.multiple_of(c * HALF, HALF), HALF)], wh, wsem)
    w_copy.start()

    sub = lax.broadcasted_iota(jnp.int32, (MEM, SEG), 0)
    idx = jnp.zeros((MEM, SEG), jnp.int32)
    for m in range(MEM):
        idx = jnp.where(sub == m, idx_ref[0, m], idx)
    idxb[c] = idx
    kp[c] = k_ref[:, my_cols]
    vp[c] = v_ref[:, my_cols]
    qp[c] = q_ref[:, my_cols]
    gp[c] = g_ref[...]
    vt[...] = jnp.zeros_like(vt)

    pl.semaphore_wait(bar, 1 + (NZ - 1) + (NY - 1) + (NX - 1))

    swaps = [
        remote(idxb.at[c], idxb.at[c], C_IDX, 0, 0, at_core()),
        remote(k_ref.at[:, their_cols], kp.at[c], C_K, 0, 0, at_core()),
        remote(v_ref.at[:, their_cols], vp.at[c], C_V, 0, 0, at_core()),
        remote(q_ref.at[:, their_cols], qp.at[c], C_Q, 0, 0, at_core()),
        remote(g_ref, gp.at[c], C_G, 0, 0, at_core()),
    ]
    for s in swaps:
        s.start()
    for s in swaps[:3]:
        s.wait_recv()

    lane = lax.broadcasted_iota(jnp.int32, (MEM, SEG), 1)
    zero = jnp.zeros((MEM, SEG), F32)
    one_a = jnp.where(idxb[0] == lane, 1.0, 0.0).astype(F32)
    one_b = jnp.where(idxb[1] == lane, 1.0, 0.0).astype(F32)
    oh[...] = jnp.concatenate(
        [jnp.concatenate([one_a, zero], 1), jnp.concatenate([zero, one_b], 1)], 0
    ).astype(BF16)
    k_pair = kp[...].reshape(2 * SEG, HALF)
    v_pair = vp[...].reshape(2 * SEG, HALF)
    kbuf[y, blk(z)] = nn(oh[...], k_pair).astype(BF16)
    vbuf[y, blk(z)] = nn(oh[...], v_pair).astype(BF16)

    each(NZ, z, lambda i: remote(kbuf.at[y, blk(z)], kbuf.at[y, blk(z)], KZ, i, z, at_z(i)).start())
    span(y + 1, NY, lambda i: remote(vbuf.at[y, blk(z)], vbuf.at[y, blk(z)], VY, i, y, at_y(i)).start())

    swaps[3].wait_recv()
    lanes = lax.broadcasted_iota(jnp.int32, (2 * SEG, HALF), 1) // HEAD_DIM
    q_pair = (qp[...].reshape(2 * SEG, HALF).astype(F32) * (1.0 / math.sqrt(HEAD_DIM))).astype(BF16)
    for h in range(HEADS):
        q4[pl.ds(h * 256, 256), :] = jnp.where(lanes == h, q_pair, jnp.zeros_like(q_pair))

    def score_block(keys):
        return nt(keys, q4[...])

    col = lax.broadcasted_iota(jnp.int32, (2 * SEG, COLS), 1)
    row = lax.broadcasted_iota(jnp.int32, (2 * SEG, COLS), 0)
    s = score_block(k_pair)
    s = jnp.where((row // SEG) == ((col // SEG) % 2), s, -jnp.inf)
    s_loc[...] = s
    m8[...] = rows8(s, jnp.max)

    swaps[4].wait_recv()
    w_copy.wait()
    g_pair = gp[...].reshape(2 * SEG, D)
    ga = nt(g_pair, wh[...]).astype(BF16)
    gat[...] = nt(wh[...], g_pair).astype(BF16).astype(F32)
    for h in range(HEADS):
        ga4[pl.ds(h * 256, 256), :] = jnp.where(lanes == h, ga, jnp.zeros_like(ga))

    each(NZ, z, lambda i: remote(kbuf.at[y, blk(z)], kbuf.at[y, blk(i)], KZ, i, i, at_z(i)).wait_recv())
    span(y + 1, NY, lambda i: remote(kbuf.at[y], kbuf.at[y], KY, i, y, at_y(i)).start())
    span(0, y, lambda i: remote(vbuf.at[y, blk(z)], vbuf.at[i, blk(z)], VY, i, i, at_y(i)).wait_recv())
    each(NZ, z, lambda i: remote(vbuf.at[:, blk(z)], vbuf.at[:, blk(z)], VZ, i, z, at_z(i)).start())

    def masked(block):
        at = lax.broadcasted_iota(jnp.int32, (SEG, COLS), 0) // MEM
        seg = 2 * z + (lax.broadcasted_iota(jnp.int32, (SEG, COLS), 1) // SEG) % 2
        return jnp.where(at < seg, block, -jnp.inf)

    s = masked(score_block(kbuf[y]))
    s_mem[y] = s
    m8[...] = jnp.maximum(m8[...], rows8(s, jnp.max))

    def scores_of(d):
        i = y - 1 - d
        remote(kbuf.at[y], kbuf.at[i], KY, i, i, at_y(i)).wait_recv()
        block = score_block(kbuf[i])
        s_mem[i] = block
        m8[...] = jnp.maximum(m8[...], rows8(block, jnp.max))

    span(0, y, scores_of)
    top = jnp.max(m8[...], axis=0, keepdims=True)

    def add_attended(values, p):
        p_low = p.astype(BF16)
        vals_t = values.T
        for h in range(HEADS):
            rows = pl.ds(h * HEAD_DIM, HEAD_DIM)
            acc[rows, :] = acc[rows, :] + nn(
                vals_t[h * HEAD_DIM : (h + 1) * HEAD_DIM], p_low[:, h * 256 : (h + 1) * 256]
            )

    p = jnp.exp(s_loc[...] - top)
    s_loc[...] = p
    l8[...] = rows8(p, jnp.sum)
    acc[...] = jnp.zeros_like(acc)
    add_attended(v_pair, p)
    each(NZ, z, lambda i: remote(vbuf.at[:, blk(z)], vbuf.at[:, blk(i)], VZ, i, i, at_z(i)).wait_recv())

    def soft_of(i):
        p = jnp.exp(s_mem[i] - top)
        s_mem[i] = p
        l8[...] = l8[...] + rows8(p, jnp.sum)
        add_attended(vbuf[i], p)

    span(0, y + 1, soft_of)
    inv = 1.0 / jnp.sum(l8[...], axis=0, keepdims=True)
    att = jnp.concatenate(
        [acc[h * HEAD_DIM : (h + 1) * HEAD_DIM, :] * inv[:, h * 256 : (h + 1) * 256] for h in range(HEADS)], 0
    ).astype(BF16)
    term = nn(att, g_pair)
    wt[...] = term
    wsend[...] = term.astype(BF16)

    def wrows(i):
        return pl.ds(pl.multiple_of(i * 64, 64), 64)

    each(NX, dp, lambda i: remote(wsend.at[wrows(i)], wxr.at[dp], WX, i, dp, at_x(i)).start())

    prod = att.astype(F32) * gat[...]
    delta = jnp.concatenate(
        [jnp.sum(prod[h * HEAD_DIM : (h + 1) * HEAD_DIM, :], axis=0, keepdims=True) for h in range(HEADS)], 1
    )

    def back(keys, values, p):
        pn = p * inv
        soft = nt(values, ga4[...])
        gs = (pn * (soft - delta)).astype(BF16)
        k_term = nn(gs, q4[...])
        v_term = nn(pn.astype(BF16), ga4[...])
        keys_t = keys.T
        for h in range(HEADS):
            rows = pl.ds(h * HEAD_DIM, HEAD_DIM)
            qacc[rows, :] = qacc[rows, :] + nn(
                keys_t[h * HEAD_DIM : (h + 1) * HEAD_DIM], gs[:, h * 256 : (h + 1) * 256]
            )
        return k_term, v_term

    qacc[...] = jnp.zeros_like(qacc)

    def back_of(i):
        k_term, v_term = back(kbuf[i], vbuf[i], s_mem[i])
        kt[i] = k_term.astype(BF16)
        vt[i] = v_term.astype(BF16)
        remote(kt.at[i], kry.at[y], RKY, i, y, at_y(i)).start()

    span(0, y, back_of)
    k_term, v_term = back(kbuf[y], vbuf[y], s_mem[y])
    kt_own[...] = k_term
    vt[y] = v_term.astype(BF16)
    each(NZ, z, lambda i: remote(vt.at[:, blk(i)], vrz.at[z], RVZ, i, z, at_z(i)).start())
    k_term, v_term = back(k_pair, v_pair, s_loc[...])
    kg[...] = k_term
    vg[...] = v_term
    qg = (qacc[...] * (1.0 / math.sqrt(HEAD_DIM))).T.astype(BF16)
    obq[...] = qg.reshape(2, SEG, HALF)
    qo_ref[:, my_cols] = obq[c]
    out_q = remote(obq.at[other], qo_ref.at[:, my_cols], O_Q, 0, 0, at_core())
    out_q.start()

    def add_x(i):
        remote(wsend.at[wrows(i)], wxr.at[i], WX, i, i, at_x(i)).wait_recv()
        wt[wrows(dp), :] = wt[wrows(dp), :] + wxr[i].astype(F32)

    each(NX, dp, add_x)
    wxs[...] = wt[wrows(dp), :].astype(BF16)

    def wcols(i):
        return pl.ds(pl.multiple_of(i * 128, 128), 128)

    each(NY, y, lambda i: remote(wxs.at[:, wcols(i)], wyr.at[y], WY, i, y, at_y(i)).start())

    ksum[...] = kt_own[...]

    def add_ky(i):
        remote(kt.at[0], kry.at[i], RKY, 0, i, at_y(i)).wait_recv()
        ksum[...] = ksum[...] + kry[i].astype(F32)

    span(y + 1, NY, add_ky)
    krow[...] = ksum[...].astype(BF16)
    each(NZ, z, lambda i: remote(krow.at[blk(i)], krz.at[z], RKZ, i, z, at_z(i)).start())

    vsum[...] = vt[:, blk(z)].astype(F32)

    def add_vz(i):
        remote(vt.at[:, blk(i)], vrz.at[i], RVZ, i, i, at_z(i)).wait_recv()
        vsum[...] = vsum[...] + vrz[i].astype(F32)

    each(NZ, z, add_vz)
    vrow[...] = vsum[...].astype(BF16)
    span(0, y, lambda i: remote(vrow.at[i], vry.at[y], RVY, i, y, at_y(i)).start())

    wys[...] = wt[wrows(dp), wcols(y)]

    def add_y(i):
        remote(wxs.at[:, wcols(i)], wyr.at[i], WY, i, i, at_y(i)).wait_recv()
        wys[...] = wys[...] + wyr[i].astype(F32)

    each(NY, y, add_y)

    def w8(i):
        return pl.ds(pl.multiple_of(i * 8, 8), 8)

    each(NZ, z, lambda i: remote(wys.at[w8(i)], wzr.at[z], WZ, i, z, at_z(i)).start())

    vsum_own[...] = vsum[y]

    def add_vy(i):
        remote(vrow.at[0], vry.at[i], RVY, 0, i, at_y(i)).wait_recv()
        vsum_own[...] = vsum_own[...] + vry[i].astype(F32)

    span(y + 1, NY, add_vy)
    kown = ksum.at[blk(z)]

    def add_kz(i):
        remote(krow.at[blk(i)], krz.at[i], RKZ, i, i, at_z(i)).wait_recv()
        kown[...] = kown[...] + krz[i].astype(F32)

    each(NZ, z, add_kz)

    def place(local, terms):
        hi = terms.astype(BF16)
        lo = (terms - hi.astype(F32)).astype(BF16)
        return (local + (tn(oh[...], hi) + tn(oh[...], lo))).astype(BF16).reshape(2, SEG, HALF)

    obk[...] = place(kg[...], kown[...])
    obv[...] = place(vg[...], vsum_own[...])
    out_k = remote(obk.at[other], ko_ref.at[:, my_cols], O_K, 0, 0, at_core())
    out_v = remote(obv.at[other], vo_ref.at[:, my_cols], O_V, 0, 0, at_core())
    out_k.start()
    out_v.start()
    ko_ref[:, my_cols] = obk[c]
    vo_ref[:, my_cols] = obv[c]

    wfin = wys.at[w8(z)]

    def add_z(i):
        remote(wys.at[w8(i)], wzr.at[i], WZ, i, i, at_z(i)).wait_recv()
        wfin[...] = wfin[...] + wzr[i]

    each(NZ, z, add_z)
    wg[w8(z), :] = wfin[...] * (1.0 / math.sqrt(4 * 16384))

    each(NZ, z, lambda i: remote(wg.at[w8(z)], wg.at[w8(z)], GZ, i, z, at_z(i)).start())
    each(NZ, z, lambda i: remote(wg.at[w8(z)], wg.at[w8(i)], GZ, i, i, at_z(i)).wait_recv())

    def orows(i):
        return pl.ds(pl.multiple_of(c * HALF + i * 64, 64), 64)

    wo_ref[orows(dp), wcols(y)] = wg[...].astype(BF16)
    here = wo_ref.at[orows(dp), wcols(y)]
    each(NY, y, lambda i: remote(here, here, GY, i, y, at_y(i)).start())
    each(NY, y, lambda i: remote(here, wo_ref.at[orows(dp), wcols(i)], GY, i, i, at_y(i)).wait_recv())
    mine = wo_ref.at[orows(dp)]
    each(NX, dp, lambda i: remote(mine, mine, GX, i, dp, at_x(i)).start())
    remote(mine, mine, GC, dp, dp, at_core()).start()

    def hand_on(i):
        part = wo_ref.at[orows(i)]
        remote(mine, part, GX, i, i, at_x(i)).wait_recv()
        remote(part, part, GC, i, i, at_core()).start()

    each(NX, dp, hand_on)

    def theirs(i):
        return wo_ref.at[pl.ds(pl.multiple_of(other * HALF + i * 64, 64), 64)]

    span(0, NX, lambda i: remote(theirs(i), theirs(i), GC, i, i, at_core()).wait_recv())

    out_q.wait()
    out_k.wait()
    out_v.wait()
    for s in swaps:
        s.wait_send()
    each(NZ, z, lambda i: remote(kbuf.at[y, blk(z)], kbuf.at[y, blk(z)], KZ, i, z, at_z(i)).wait_send())
    span(y + 1, NY, lambda i: remote(vbuf.at[y, blk(z)], vbuf.at[y, blk(z)], VY, i, y, at_y(i)).wait_send())
    span(y + 1, NY, lambda i: remote(kbuf.at[y], kbuf.at[y], KY, i, y, at_y(i)).wait_send())
    each(NZ, z, lambda i: remote(vbuf.at[:, blk(z)], vbuf.at[:, blk(z)], VZ, i, z, at_z(i)).wait_send())
    each(NX, dp, lambda i: remote(wsend.at[wrows(i)], wxr.at[dp], WX, i, dp, at_x(i)).wait_send())
    span(0, y, lambda i: remote(kt.at[i], kry.at[y], RKY, i, y, at_y(i)).wait_send())
    each(NZ, z, lambda i: remote(vt.at[:, blk(i)], vrz.at[z], RVZ, i, z, at_z(i)).wait_send())
    each(NY, y, lambda i: remote(wxs.at[:, wcols(i)], wyr.at[y], WY, i, y, at_y(i)).wait_send())
    each(NZ, z, lambda i: remote(krow.at[blk(i)], krz.at[z], RKZ, i, z, at_z(i)).wait_send())
    span(0, y, lambda i: remote(vrow.at[i], vry.at[y], RVY, i, y, at_y(i)).wait_send())
    each(NZ, z, lambda i: remote(wys.at[w8(i)], wzr.at[z], WZ, i, z, at_z(i)).wait_send())
    each(NZ, z, lambda i: remote(wg.at[w8(z)], wg.at[w8(z)], GZ, i, z, at_z(i)).wait_send())
    each(NY, y, lambda i: remote(here, here, GY, i, y, at_y(i)).wait_send())
    each(NX, dp, lambda i: remote(mine, mine, GX, i, dp, at_x(i)).wait_send())
    span(0, NX, lambda i: remote(wo_ref.at[orows(i)], wo_ref.at[orows(i)], GC, i, i, at_core()).wait_send())


def on_device(query_rows, key_rows, value_rows, out_grad, out_weight, memory_index):
    vmem = pl.BlockSpec(memory_space=pltpu.VMEM)
    V = pltpu.VMEM
    scratch = [
        V((2, MEM, SEG), jnp.int32),
        V((2, SEG, HALF), BF16), V((2, SEG, HALF), BF16), V((2, SEG, HALF), BF16),
        V((2, SEG, D), BF16), V((HALF, D), BF16),
        V((COLS, HALF), BF16), V((COLS, HALF), BF16), V((HALF, HALF), F32),
        V((16, HALF), BF16),
        V((NY, SEG, HALF), BF16), V((NY, SEG, HALF), BF16),
        V((NY, SEG, COLS), F32), V((2 * SEG, COLS), F32),
        V((8, COLS), F32), V((8, COLS), F32),
        V((HALF, HALF), F32), V((HALF, HALF), F32),
        V((NY, SEG, HALF), BF16), V((NY, SEG, HALF), BF16), V((SEG, HALF), F32),
        V((HALF, HALF), F32), V((HALF, HALF), F32),
        V((NY, SEG, HALF), BF16), V((NZ, 16, HALF), BF16),
        V((NZ, NY, 16, HALF), BF16), V((NY, 16, HALF), BF16),
        V((SEG, HALF), F32), V((NY, 16, HALF), F32), V((16, HALF), F32),
        V((SEG, HALF), BF16), V((NY, 16, HALF), BF16),
        V((HALF, D), F32), V((HALF, D), BF16),
        V((NX, 64, D), BF16), V((64, D), BF16),
        V((NY, 64, 128), BF16), V((64, 128), F32),
        V((NZ, 8, 128), F32), V((64, 128), F32),
        V((2, SEG, HALF), BF16), V((2, SEG, HALF), BF16), V((2, SEG, HALF), BF16),
        pltpu.SemaphoreType.DMA((23, 8)), pltpu.SemaphoreType.DMA((23, 8)), pltpu.SemaphoreType.DMA(()),
    ]
    qg, kgrad, vgrad, wgrad = pl.pallas_call(
        kernel,
        out_shape=(
            jax.ShapeDtypeStruct((SEG, HD), BF16),
            jax.ShapeDtypeStruct((SEG, HD), BF16),
            jax.ShapeDtypeStruct((SEG, HD), BF16),
            jax.ShapeDtypeStruct((HD, D), BF16),
        ),
        in_specs=[pl.BlockSpec(memory_space=pltpu.SMEM), vmem, vmem, vmem, vmem, pl.BlockSpec(memory_space=pl.ANY)],
        out_specs=(vmem, vmem, vmem, vmem),
        scratch_shapes=scratch,
        compiler_params=pltpu.CompilerParams(
            collective_id=0, has_side_effects=True, vmem_limit_bytes=48 * 2**20
        ),
        name="memory_attention_backward",
    )(memory_index[0], query_rows[0], key_rows[0], value_rows[0], out_grad[0], out_weight)
    return qg[None], kgrad[None], vgrad[None], wgrad


def solution(mesh):
    placed = (
        P("dp", "tm", None),
        P("dp", "tm", None),
        P("dp", "tm", None),
        P("dp", "tm", None),
        P(),
        P("dp", "tm", None),
    )
    return jax.shard_map(
        on_device,
        mesh=mesh,
        in_specs=placed,
        out_specs=(P("dp", "tm", None), P("dp", "tm", None), P("dp", "tm", None), P()),
        check_vma=False,
    )
```

time: 941 us -> 94.4 us (0.10)
  waiting for transfers between devices: 813 us -> 0 us
  Pallas kernels: 0 us -> 85.1 us
  matrix products: 51.1 us -> 0 us
  local copies, waits for them, and re-layouts: 39.1 us -> 8.47 us
  other arithmetic: 16.1 us -> 0 us
  between operations: 13.9 us -> 0.66 us
    reduce_scatter x2 -> x0, waiting for transfers between devices: 392 us -> none  [the longest x1 199 us: on_device(): lax.psum_scatter(slot_keys, 'tm', scatter_dimension=0, tiled=True)]
    psum x1 -> x0, waiting for transfers between devices: 264 us -> none  [on_device(): summed = lax.psum(weight_term, ('dp', 'tm'))]
    all_gather x2 -> x0, waiting for transfers between devices: 155 us -> none  [the longest x1 78.8 us: on_device(): lax.all_gather(own_values, 'tm', axis=0, tiled=True)]
    pallas_call x0 -> x1, Pallas kernels: none -> 85.1 us  [on_device(): pl.pallas_call(kernel, out_shape=(jax.ShapeDtypeStruct((SEG, HD), BF16),...]
    dot_general x50 -> x0, matrix products: 51.1 us -> none  [the longest x8 14 us: head_pass(): jnp.dot(soft_low.T, grad_head, preferred_element_type=jnp.float32)]
    dynamic_slice x48 -> x0, local copies, waits for them, and re-layouts: 17.9 us -> none  [on_device(): lax.map(per_head, (split_heads(query_seg), split_heads(key_seg), split_he...]
  transfers between devices with their start and end apart: 5 -> 0, of which waited for: 5 -> 0; matrix products, arithmetic and copies ran while one was open for 2% -> 0% of each run, Pallas kernels for 0% -> 0%
where the time goes in v1:
time: 94.4 us; the launch traced here: 94.2 us
  Pallas kernels  85.1 us (90%)
  local copies, waits for them, and re-layouts  8.47 us (9%)
    pallas_call x1, Pallas kernels, on_device(): pl.pallas_call(kernel, out_shape=(jax.ShapeDtypeStruct((SEG, HD), BF16),...  85.1 us
    unnamed x16, local copies, waits for them, and re-layouts  8.47 us

profile of v1, /device:TPU:1, one launch (start us, length us, event | category | flops | bytes accessed | tf_op | source)
XLA Modules:
  0.0 94.2 jit_solution(3875394162296666387)
XLA Ops:
  0.6 0.0 copy-start.5
  0.6 0.6 copy-done.5
  1.3 0.0 copy-start
  1.3 1.2 %copy-done = bf16[512,1024]{1,0:T(8,128)(2,1)S(1)} copy-done((bf16[512,1024]{1,0:T(8,128)(2,1)S(1)}, bf16[512,1024]{1,0:T(8,128)(2,1)}, u32[]{:S(2)}) %copy-start) | copy-done | bytes 1048600
  2.5 0.0 copy-start.1
  2.5 0.9 %copy-done.1 = bf16[1,128,1024]{2,1,0:T(8,128)(2,1)S(1)} copy-done((bf16[1,128,1024]{2,1,0:T(8,128)(2,1)S(1)}, bf16[1,128,1024]{2,1,0:T(8,128)(2,1)}, u32[]{:S(2)}) %copy-start.1) | copy-done | bytes 262168
  3.5 0.0 copy-start.2
  3.5 0.9 copy-done.2
  4.4 0.0 copy-start.3
  4.4 0.9 copy-done.3
  5.3 0.0 copy-start.4
  5.3 0.9 copy-done.4
  6.2 85.1 %memory_attention_backward.1 = (bf16[128,512]{1,0:T(8,128)(2,1)S(1)}, bf16[128,512]{1,0:T(8,128)(2,1)S(1)}, bf16[128,512]{1,0:T(8,128)(2,1)S(1)}, bf16[512,1024]{1,0:T(8,128)(2,1)S(1)}) custom-call(s32[1,8]{1,0:T(1,128)S(1)} %bitcast.15, bf16[128,512]{1,0:T(8,128)(2,1)S(1)} %bitcast.9, bf16[128,512]{1,0:T(8,128)(2,1)S(1)} %bitcast.10, ...), custom_call_target="tpu_custom_call" | custom-call | tf_op jit(solution)/shard_map/memory_attention_backward/pallas_call | solution.py:428
  91.3 0.7 copy.14
  91.9 0.7 copy.15
  92.6 0.7 copy.16
  93.2 1.0 %copy.17 = bf16[512,1024]{1,0:T(8,128)(2,1)} copy(bf16[512,1024]{1,0:T(8,128)(2,1)S(1)} %get-tuple-element.19) | data formatting | bytes 2097152
Async XLA Ops:
  0.6 0.7 copy-start.5
  1.3 1.2 %copy-start = (bf16[512,1024]{1,0:T(8,128)(2,1)S(1)}, bf16[512,1024]{1,0:T(8,128)(2,1)}, u32[]{:S(2)}) copy-start(bf16[512,1024]{1,0:T(8,128)(2,1)} %w_ref.1) | copy-start | bytes 3145732
  2.5 0.9 %copy-start.1 = (bf16[1,128,1024]{2,1,0:T(8,128)(2,1)S(1)}, bf16[1,128,1024]{2,1,0:T(8,128)(2,1)}, u32[]{:S(2)}) copy-start(bf16[1,128,1024]{2,1,0:T(8,128)(2,1)} %param.9) | copy-start | bytes 786436
  3.5 0.9 copy-start.2
  4.4 0.9 copy-start.3
  5.3 0.9 copy-start.4

commit v2 on v1

v2 whole, which is shorter than its diff:
```python
import math

import jax
import jax.numpy as jnp
from jax import lax
from jax.experimental import pallas as pl
from jax.experimental.pallas import tpu as pltpu
from jax.sharding import PartitionSpec as P

HEAD_DIM = 64
SEG = 128
MEM = 8
HD = 512
D = 1024
HALF = 256
HEADS = 4
COLS = HEADS * 2 * SEG
NY, NZ, NX = 8, 8, 4
MESH = pl.DeviceIdType.MESH
F32, BF16 = jnp.float32, jnp.bfloat16

(
    C_IDX, C_K, C_V, C_Q, C_G, KZ, KU, KU1, KD, KD1, VY, VU, VU1, VD, VD1,
    RKY, RKZ, RVZ, RVZ1, RVY, WX, WY, WZ, GY, GC, GD, O_Q, O_K, O_V, GX,
) = range(30)
PHASES = GX + NX


def nt(a, b):
    return lax.dot_general(a, b, (((1,), (1,)), ((), ())), preferred_element_type=F32)


def tn(a, b):
    return lax.dot_general(a, b, (((0,), (0,)), ((), ())), preferred_element_type=F32)


def nn(a, b):
    return jnp.dot(a, b, preferred_element_type=F32)


def rows8(block, op):
    return op(block.reshape(block.shape[0] // 8, 8, block.shape[1]), axis=0)


def kernel(
    idx_in, q_ref, k_ref, v_ref, g_ref, w_ref,
    qo_ref, ko_ref, vo_ref, wout_ref,
    idx_ref, idxb, kp, vp, qp, gp, wh, q4, ga4, gat, oh, kbuf, vbuf, s_mem, s_loc,
    m8, l8, acc, qacc, kt, vt, kg, vg, kry, krz, vrz, vry, ksum, vsum, vsum_own, krow, vrow,
    wt, wsend, wxr, wxs, wyr, wys, wzr, wo_ref, obq, obk, obv,
    ssem, rsem, lsem,
):
    dp, tm = lax.axis_index("dp"), lax.axis_index("tm")
    c, z, y = tm % 2, (tm // 2) % NZ, tm // (2 * NZ)
    other = 1 - c

    def at_core():
        return (dp, y * 16 + z * 2 + other)

    def at_z(i):
        return (dp, y * 16 + i * 2 + c)

    def at_y(i):
        return (dp, i * 16 + z * 2 + c)

    def at_x(i):
        return (i, tm)

    def remote(src, dst, phase, mine, theirs, device):
        return pltpu.make_async_remote_copy(
            src_ref=src, dst_ref=dst, send_sem=ssem.at[phase, mine], recv_sem=rsem.at[phase, theirs],
            device_id=device, device_id_type=MESH,
        )

    def each(count, me, body):
        def step(d, _):
            body((me + d) % count)
            return 0

        lax.fori_loop(1, count, step, 0)

    def span(lo, hi, body):
        def step(i, _):
            body(i)
            return 0

        lax.fori_loop(lo, hi, step, 0)

    def blk(i):
        return pl.ds(pl.multiple_of(i * 16, 16), 16)

    my_cols = pl.ds(pl.multiple_of(c * HALF, HALF), HALF)
    their_cols = pl.ds(pl.multiple_of(other * HALF, HALF), HALF)

    kbuf[...] = jnp.zeros_like(kbuf)
    vbuf[...] = jnp.zeros_like(vbuf)

    local = [
        pltpu.make_async_copy(src, dst, lsem.at[i])
        for i, (src, dst) in enumerate((
            (idx_in.at[0], idx_ref),
            (k_ref.at[:, my_cols], kp.at[c]),
            (v_ref.at[:, my_cols], vp.at[c]),
            (q_ref.at[:, my_cols], qp.at[c]),
            (g_ref, gp.at[c]),
            (w_ref.at[pl.ds(pl.multiple_of(c * HALF, HALF), HALF)], wh),
        ))
    ]
    for copy in local:
        copy.start()

    bar = pltpu.get_barrier_semaphore()

    def greet(device):
        pl.semaphore_signal(bar, inc=1, device_id=device, device_id_type=MESH)

    greet(at_core())
    each(NZ, z, lambda i: greet(at_z(i)))
    each(NY, y, lambda i: greet(at_y(i)))
    each(NX, dp, lambda i: greet(at_x(i)))

    vt[...] = jnp.zeros_like(vt)
    pl.semaphore_wait(bar, 1 + (NZ - 1) + (NY - 1) + (NX - 1))

    swaps = [
        remote(idxb.at[c], idxb.at[c], C_IDX, 0, 0, at_core()),
        remote(k_ref.at[:, their_cols], kp.at[c], C_K, 0, 0, at_core()),
        remote(v_ref.at[:, their_cols], vp.at[c], C_V, 0, 0, at_core()),
        remote(q_ref.at[:, their_cols], qp.at[c], C_Q, 0, 0, at_core()),
        remote(g_ref, gp.at[c], C_G, 0, 0, at_core()),
    ]
    swaps[1].start()
    swaps[2].start()
    local[0].wait()
    sub = lax.broadcasted_iota(jnp.int32, (MEM, SEG), 0)
    idx = jnp.zeros((MEM, SEG), jnp.int32)
    for m in range(MEM):
        idx = jnp.where(sub == m, idx_ref[m], idx)
    idxb[c] = idx
    swaps[0].start()
    swaps[3].start()
    swaps[4].start()
    local[1].wait()
    local[2].wait()
    for s in swaps[:3]:
        s.wait_recv()

    lane = lax.broadcasted_iota(jnp.int32, (MEM, SEG), 1)
    zero = jnp.zeros((MEM, SEG), F32)
    one_a = jnp.where(idxb[0] == lane, 1.0, 0.0).astype(F32)
    one_b = jnp.where(idxb[1] == lane, 1.0, 0.0).astype(F32)
    oh[...] = jnp.concatenate(
        [jnp.concatenate([one_a, zero], 1), jnp.concatenate([zero, one_b], 1)], 0
    ).astype(BF16)
    k_pair = kp[...].reshape(2 * SEG, HALF)
    v_pair = vp[...].reshape(2 * SEG, HALF)
    kbuf[y, blk(z)] = nn(oh[...], k_pair).astype(BF16)
    vbuf[y, blk(z)] = nn(oh[...], v_pair).astype(BF16)

    each(NZ, z, lambda i: remote(kbuf.at[y, blk(z)], kbuf.at[y, blk(z)], KZ, i, z, at_z(i)).start())
    span(y + 1, NY, lambda i: remote(vbuf.at[y, blk(z)], vbuf.at[y, blk(z)], VY, i, y, at_y(i)).start())

    local[3].wait()
    swaps[3].wait_recv()
    lanes = lax.broadcasted_iota(jnp.int32, (2 * SEG, HALF), 1) // HEAD_DIM
    q_pair = (qp[...].reshape(2 * SEG, HALF).astype(F32) * (1.0 / math.sqrt(HEAD_DIM))).astype(BF16)
    for h in range(HEADS):
        q4[pl.ds(h * 256, 256), :] = jnp.where(lanes == h, q_pair, jnp.zeros_like(q_pair))

    def score_block(keys):
        return nt(keys, q4[...])

    col = lax.broadcasted_iota(jnp.int32, (2 * SEG, COLS), 1)
    row = lax.broadcasted_iota(jnp.int32, (2 * SEG, COLS), 0)
    s = score_block(k_pair)
    s = jnp.where((row // SEG) == ((col // SEG) % 2), s, -jnp.inf)
    s_loc[...] = s
    m8[...] = rows8(s, jnp.max)

    local[4].wait()
    local[5].wait()
    swaps[4].wait_recv()
    g_pair = gp[...].reshape(2 * SEG, D)
    ga = nt(g_pair, wh[...]).astype(BF16)
    gat[...] = nt(wh[...], g_pair).astype(BF16).astype(F32)
    for h in range(HEADS):
        ga4[pl.ds(h * 256, 256), :] = jnp.where(lanes == h, ga, jnp.zeros_like(ga))

    each(NZ, z, lambda i: remote(kbuf.at[y, blk(z)], kbuf.at[y, blk(i)], KZ, i, i, at_z(i)).wait_recv())

    up_y, dn_y, up_z, dn_z = (y + 1) % NY, (y + NY - 1) % NY, (z + 1) % NZ, (z + NZ - 1) % NZ

    def k_pass(phase, device, b, part):
        ref = kbuf.at[b, pl.ds(part * 64, 64)]
        return remote(ref, ref, phase + part, b, b, device)

    def v_pass(phase, device, b, part):
        ref = vbuf.at[pl.ds(part * 4, 4), blk(b)]
        return remote(ref, ref, phase + part, b, b, device)

    def k_up(b, part):
        return k_pass(KU, at_y(up_y), b, part)

    def k_dn(b, part):
        return k_pass(KD, at_y(dn_y), b, part)

    def v_up(b, part):
        return v_pass(VU, at_z(up_z), b, part)

    def v_dn(b, part):
        return v_pass(VD, at_z(dn_z), b, part)

    def begin(copy, b):
        copy(b, 0).start()
        copy(b, 1).start()

    def hand_on(copy, b, more):
        for part in range(2):
            copy(b, part).wait_recv()

            @pl.when(more)
            def _():
                copy(b, part).start()

    @pl.when(y < NY - 1)
    def _():
        begin(k_up, y)

    @pl.when(y <= 2)
    def _():
        begin(k_dn, y)

    span(0, y, lambda i: remote(vbuf.at[y, blk(z)], vbuf.at[i, blk(z)], VY, i, i, at_y(i)).wait_recv())
    begin(v_up, z)
    begin(v_dn, z)

    def masked(block):
        at = lax.broadcasted_iota(jnp.int32, (SEG, COLS), 0) // MEM
        seg = 2 * z + (lax.broadcasted_iota(jnp.int32, (SEG, COLS), 1) // SEG) % 2
        return jnp.where(at < seg, block, -jnp.inf)

    s = masked(score_block(kbuf[y]))
    s_mem[y] = s
    m8[...] = jnp.maximum(m8[...], rows8(s, jnp.max))

    def scores_of(i):
        block = score_block(kbuf[i])
        s_mem[i] = block
        m8[...] = jnp.maximum(m8[...], rows8(block, jnp.max))

    def gather_step(step):
        below, above = y - step, (y + step) % NY
        from_above = (step <= 3) & (above <= 2)

        @pl.when(below >= 0)
        def _():
            hand_on(k_up, below, (step < 4) & (y < NY - 1))

        @pl.when(from_above)
        def _():
            hand_on(k_dn, above, step < 3)

        hand_on(v_up, (z + NZ - step) % NZ, step < 4)

        @pl.when(step <= 3)
        def _():
            hand_on(v_dn, (z + step) % NZ, step < 3)

        @pl.when(below >= 0)
        def _():
            scores_of(below)

        @pl.when(from_above & (above < y))
        def _():
            scores_of(above)

    span(1, 5, gather_step)
    pairs = y // 2 + 1

    @pl.when(y % 2 == 0)
    def _():
        s_mem[y + 1] = jnp.full((SEG, COLS), -jnp.inf, F32)

    def two(i):
        return pl.ds(2 * i, 2)

    top = jnp.max(m8[...], axis=0, keepdims=True)

    def add_attended(values, p):
        p_low = p.astype(BF16)
        vals_t = values.T
        for h in range(HEADS):
            rows = pl.ds(h * HEAD_DIM, HEAD_DIM)
            acc[rows, :] = acc[rows, :] + nn(
                vals_t[h * HEAD_DIM : (h + 1) * HEAD_DIM], p_low[:, h * 256 : (h + 1) * 256]
            )

    p = jnp.exp(s_loc[...] - top)
    s_loc[...] = p
    l8[...] = rows8(p, jnp.sum)
    acc[...] = jnp.zeros_like(acc)
    add_attended(v_pair, p)

    def soft_of(i):
        p = jnp.exp(s_mem[two(i)].reshape(2 * SEG, COLS) - top)
        s_mem[two(i)] = p.reshape(2, SEG, COLS)
        l8[...] = l8[...] + rows8(p, jnp.sum)
        add_attended(vbuf[two(i)].reshape(2 * SEG, HALF), p)

    span(0, pairs, soft_of)
    inv = 1.0 / jnp.sum(l8[...], axis=0, keepdims=True)
    att = jnp.concatenate(
        [acc[h * HEAD_DIM : (h + 1) * HEAD_DIM, :] * inv[:, h * 256 : (h + 1) * 256] for h in range(HEADS)], 0
    ).astype(BF16)
    term = nn(att, g_pair)
    wt[...] = term
    wsend[...] = term.astype(BF16)

    def wrows(i):
        return pl.ds(pl.multiple_of(i * 64, 64), 64)

    each(NX, dp, lambda i: remote(wsend.at[wrows(i)], wxr.at[dp], WX, i, dp, at_x(i)).start())

    prod = att.astype(F32) * gat[...]
    delta = jnp.concatenate(
        [jnp.sum(prod[h * HEAD_DIM : (h + 1) * HEAD_DIM, :], axis=0, keepdims=True) for h in range(HEADS)], 1
    )

    def back(keys, values, p):
        pn = p * inv
        soft = nt(values, ga4[...])
        gs = (pn * (soft - delta)).astype(BF16)
        k_term = nn(gs, q4[...])
        v_term = nn(pn.astype(BF16), ga4[...])
        keys_t = keys.T
        for h in range(HEADS):
            rows = pl.ds(h * HEAD_DIM, HEAD_DIM)
            qacc[rows, :] = qacc[rows, :] + nn(
                keys_t[h * HEAD_DIM : (h + 1) * HEAD_DIM], gs[:, h * 256 : (h + 1) * 256]
            )
        return k_term, v_term

    qacc[...] = jnp.zeros_like(qacc)

    def back_of(i):
        k_term, v_term = back(
            kbuf[two(i)].reshape(2 * SEG, HALF), vbuf[two(i)].reshape(2 * SEG, HALF),
            s_mem[two(i)].reshape(2 * SEG, COLS),
        )
        kt[two(i)] = k_term.astype(BF16).reshape(2, SEG, HALF)
        vt[two(i)] = v_term.astype(BF16).reshape(2, SEG, HALF)
        for j in (2 * i, 2 * i + 1):
            @pl.when(j < y)
            def _():
                remote(kt.at[j], kry.at[y], RKY, j, y, at_y(j)).start()

        @pl.when(i == 1)
        def _():
            v_half(0)

    def v_send(half, i):
        part = pl.ds(half * 4, 4)
        return remote(vt.at[part, blk(i)], vrz.at[z, part], RVZ + half, i, z, at_z(i))

    def v_half(half):
        each(NZ, z, lambda i: v_send(half, i).start())

    span(0, pairs, back_of)

    @pl.when(y < 2)
    def _():
        v_half(0)

    @pl.when(y >= 4)
    def _():
        v_half(1)

    k_term, v_term = back(k_pair, v_pair, s_loc[...])
    kg[...] = k_term
    vg[...] = v_term
    qg = (qacc[...] * (1.0 / math.sqrt(HEAD_DIM))).T.astype(BF16)
    obq[...] = qg.reshape(2, SEG, HALF)
    out_q = remote(obq.at[other], qo_ref.at[:, my_cols], O_Q, 0, 0, at_core())
    out_q.start()
    keep_q = pltpu.make_async_copy(obq.at[c], qo_ref.at[:, my_cols], lsem.at[6])
    keep_q.start()

    def add_x(i):
        remote(wsend.at[wrows(i)], wxr.at[i], WX, i, i, at_x(i)).wait_recv()
        wt[wrows(dp), :] = wt[wrows(dp), :] + wxr[i].astype(F32)

    each(NX, dp, add_x)
    wxs[...] = wt[wrows(dp), :].astype(BF16)

    def wcols(i):
        return pl.ds(pl.multiple_of(i * 128, 128), 128)

    each(NY, y, lambda i: remote(wxs.at[:, wcols(i)], wyr.at[y], WY, i, y, at_y(i)).start())

    def add_vz(half):
        part = pl.ds(half * 4, 4)
        vsum[part] = vt[part, blk(z)].astype(F32)

        def add(i):
            v_send(half, i).wait_send()
            remote(vt.at[part, blk(i)], vrz.at[i, part], RVZ + half, i, i, at_z(i)).wait_recv()
            vsum[part] = vsum[part] + vrz[i, part].astype(F32)

        each(NZ, z, add)

    add_vz(0)

    @pl.when(y >= 4)
    def _():
        add_vz(1)

    vrow[...] = vsum[...].astype(BF16)
    span(0, y, lambda i: remote(vrow.at[i], vry.at[y], RVY, i, y, at_y(i)).start())

    wys[...] = wt[wrows(dp), wcols(y)]

    def add_y(i):
        remote(wxs.at[:, wcols(i)], wyr.at[i], WY, i, i, at_y(i)).wait_recv()
        wys[...] = wys[...] + wyr[i].astype(F32)

    each(NY, y, add_y)
    wzr[z] = wys[...].astype(BF16)
    each(NZ, z, lambda i: remote(wzr.at[z], wzr.at[z], WZ, i, z, at_z(i)).start())

    ksum[...] = kt[y].astype(F32)

    def add_ky(i):
        remote(kt.at[0], kry.at[i], RKY, 0, i, at_y(i)).wait_recv()
        ksum[...] = ksum[...] + kry[i].astype(F32)

    span(y + 1, NY, add_ky)
    krow[...] = ksum[...].astype(BF16)
    each(NZ, z, lambda i: remote(krow.at[blk(i)], krz.at[z], RKZ, i, z, at_z(i)).start())

    each(NZ, z, lambda i: remote(wzr.at[z], wzr.at[i], WZ, i, i, at_z(i)).wait_recv())
    total = wzr[0].astype(F32)
    for i in range(1, NZ):
        total = total + wzr[i].astype(F32)

    def piece(i, j):
        return wo_ref.at[wrows(i), wcols(j)]

    def out_rows(half, i):
        return wout_ref.at[pl.ds(pl.multiple_of(half * HALF + i * 64, 64), 64)]

    def out_piece(half, i, j):
        return wout_ref.at[pl.ds(pl.multiple_of(half * HALF + i * 64, 64), 64), wcols(j)]

    wo_ref[wrows(dp), wcols(y)] = (total * (1.0 / math.sqrt(4 * 16384))).astype(BF16)
    here = piece(dp, y)

    def send_x(i, j):
        return pltpu.make_async_remote_copy(
            src_ref=piece(dp, j), dst_ref=piece(dp, j), send_sem=ssem.at[GX + i, j], recv_sem=rsem.at[GX + dp, j],
            device_id=at_x(i), device_id_type=MESH,
        )

    def to_x(j):
        each(NX, dp, lambda i: send_x(i, j).start())
        remote(piece(dp, j), out_piece(c, dp, j), GC, j, j, at_core()).start()

    def keep(i):
        return pltpu.make_async_copy(wo_ref.at[wrows(i)], out_rows(c, i), lsem.at[9 + i])

    each(NY, y, lambda i: remote(here, here, GY, i, y, at_y(i)).start())
    to_x(y)

    def from_y(i):
        remote(here, piece(dp, i), GY, i, i, at_y(i)).wait_recv()
        to_x(i)

    each(NY, y, from_y)
    keep(dp).start()

    vsum_own[...] = vsum[y]

    def add_vy(i):
        remote(vrow.at[0], vry.at[i], RVY, 0, i, at_y(i)).wait_recv()
        vsum_own[...] = vsum_own[...] + vry[i].astype(F32)

    span(y + 1, NY, add_vy)
    kown = ksum.at[blk(z)]

    def add_kz(i):
        remote(krow.at[blk(i)], krz.at[i], RKZ, i, i, at_z(i)).wait_recv()
        kown[...] = kown[...] + krz[i].astype(F32)

    each(NZ, z, add_kz)

    def place(local, terms):
        hi = terms.astype(BF16)
        lo = (terms - hi.astype(F32)).astype(BF16)
        return (local + (tn(oh[...], hi) + tn(oh[...], lo))).astype(BF16).reshape(2, SEG, HALF)

    obk[...] = place(kg[...], kown[...])
    obv[...] = place(vg[...], vsum_own[...])
    out_k = remote(obk.at[other], ko_ref.at[:, my_cols], O_K, 0, 0, at_core())
    out_v = remote(obv.at[other], vo_ref.at[:, my_cols], O_V, 0, 0, at_core())
    out_k.start()
    out_v.start()
    keep_k = pltpu.make_async_copy(obk.at[c], ko_ref.at[:, my_cols], lsem.at[7])
    keep_v = pltpu.make_async_copy(obv.at[c], vo_ref.at[:, my_cols], lsem.at[8])
    keep_k.start()
    keep_v.start()

    def from_x(i):
        span(0, NY, lambda j: remote(piece(i, j), piece(i, j), GX + i, j, j, at_x(i)).wait_recv())
        remote(wo_ref.at[wrows(i)], out_rows(c, i), GD, i, i, at_core()).start()
        keep(i).start()

    each(NX, dp, from_x)
    span(0, NY, lambda j: remote(here, out_piece(other, dp, j), GC, j, j, at_core()).wait_recv())
    each(NX, dp, lambda i: remote(wo_ref.at[wrows(i)], out_rows(other, i), GD, i, i, at_core()).wait_recv())
    span(0, NX, lambda i: keep(i).wait())
    keep_q.wait()
    keep_k.wait()
    keep_v.wait()

    out_q.wait()
    out_k.wait()
    out_v.wait()
    for s in swaps:
        s.wait_send()
    each(NZ, z, lambda i: remote(kbuf.at[y, blk(z)], kbuf.at[y, blk(z)], KZ, i, z, at_z(i)).wait_send())
    span(y + 1, NY, lambda i: remote(vbuf.at[y, blk(z)], vbuf.at[y, blk(z)], VY, i, y, at_y(i)).wait_send())

    def sent(copy, b):
        copy(b, 0).wait_send()
        copy(b, 1).wait_send()

    def gather_sent(step):
        below, above = y - step, (y + step) % NY

        @pl.when((below >= 0) & (step < 4) & (y < NY - 1))
        def _():
            sent(k_up, below)

        @pl.when((step < 3) & (above <= 2))
        def _():
            sent(k_dn, above)

        sent(v_up, (z + NZ - step) % NZ)

        @pl.when(step < 3)
        def _():
            sent(v_dn, (z + step) % NZ)

    span(0, 4, gather_sent)
    each(NX, dp, lambda i: remote(wsend.at[wrows(i)], wxr.at[dp], WX, i, dp, at_x(i)).wait_send())
    span(0, y, lambda i: remote(kt.at[i], kry.at[y], RKY, i, y, at_y(i)).wait_send())
    each(NY, y, lambda i: remote(wxs.at[:, wcols(i)], wyr.at[y], WY, i, y, at_y(i)).wait_send())
    each(NZ, z, lambda i: remote(krow.at[blk(i)], krz.at[z], RKZ, i, z, at_z(i)).wait_send())
    span(0, y, lambda i: remote(vrow.at[i], vry.at[y], RVY, i, y, at_y(i)).wait_send())
    each(NZ, z, lambda i: remote(wzr.at[z], wzr.at[z], WZ, i, z, at_z(i)).wait_send())
    each(NY, y, lambda i: remote(here, here, GY, i, y, at_y(i)).wait_send())
    span(0, NY, lambda j: remote(piece(dp, j), out_piece(c, dp, j), GC, j, j, at_core()).wait_send())

    def x_sent(i):
        span(0, NY, lambda j: send_x(i, j).wait_send())
        remote(wo_ref.at[wrows(i)], out_rows(c, i), GD, i, i, at_core()).wait_send()

    each(NX, dp, x_sent)


def store(*refs):
    arrays, outs, held, sem = refs[:4], refs[4:8], refs[8:12], refs[12]
    loads = [pltpu.make_async_copy(arrays[i], held[i], sem.at[0, i]) for i in range(4)]
    stores = [pltpu.make_async_copy(held[i], outs[i], sem.at[1, i]) for i in range(4)]
    for copy in loads:
        copy.start()
    for load, copy in zip(loads, stores):
        load.wait()
        copy.start()
    for copy in stores:
        copy.wait()


def on_device(query_rows, key_rows, value_rows, out_grad, out_weight, memory_index):
    V = pltpu.VMEM
    scratch = [
        pltpu.SMEM((MEM,), jnp.int32), V((2, MEM, SEG), jnp.int32),
        V((2, SEG, HALF), BF16), V((2, SEG, HALF), BF16), V((2, SEG, HALF), BF16),
        V((2, SEG, D), BF16), V((HALF, D), BF16),
        V((COLS, HALF), BF16), V((COLS, HALF), BF16), V((HALF, HALF), F32),
        V((16, HALF), BF16),
        V((NY, SEG, HALF), BF16), V((NY, SEG, HALF), BF16),
        V((NY, SEG, COLS), F32), V((2 * SEG, COLS), F32),
        V((8, COLS), F32), V((8, COLS), F32),
        V((HALF, HALF), F32), V((HALF, HALF), F32),
        V((NY, SEG, HALF), BF16), V((NY, SEG, HALF), BF16),
        V((HALF, HALF), F32), V((HALF, HALF), F32),
        V((NY, SEG, HALF), BF16), V((NZ, 16, HALF), BF16),
        V((NZ, NY, 16, HALF), BF16), V((NY, 16, HALF), BF16),
        V((SEG, HALF), F32), V((NY, 16, HALF), F32), V((16, HALF), F32),
        V((SEG, HALF), BF16), V((NY, 16, HALF), BF16),
        V((HALF, D), F32), V((HALF, D), BF16),
        V((NX, 64, D), BF16), V((64, D), BF16),
        V((NY, 64, 128), BF16), V((64, 128), F32),
        V((NZ, 64, 128), BF16), V((HALF, D), BF16),
        V((2, SEG, HALF), BF16), V((2, SEG, HALF), BF16), V((2, SEG, HALF), BF16),
        pltpu.SemaphoreType.DMA((PHASES, 8)), pltpu.SemaphoreType.DMA((PHASES, 8)), pltpu.SemaphoreType.DMA((9 + NX,)),
    ]
    qg, kgrad, vgrad, wgrad = pl.pallas_call(
        kernel,
        out_shape=(
            jax.ShapeDtypeStruct((SEG, HD), BF16),
            jax.ShapeDtypeStruct((SEG, HD), BF16),
            jax.ShapeDtypeStruct((SEG, HD), BF16),
            jax.ShapeDtypeStruct((HD, D), BF16),
        ),
        in_specs=[pl.BlockSpec(memory_space=pltpu.HBM)] * 6,
        out_specs=[pl.BlockSpec(memory_space=pltpu.HBM)] * 4,
        scratch_shapes=scratch,
        compiler_params=pltpu.CompilerParams(
            collective_id=0, has_side_effects=True, vmem_limit_bytes=64 * 2**20
        ),
        name="memory_attention_backward",
    )(memory_index[0], query_rows[0], key_rows[0], value_rows[0], out_grad[0], out_weight)
    qg, kgrad, vgrad, wgrad = pl.pallas_call(
        store,
        out_shape=tuple(jax.ShapeDtypeStruct(a.shape, a.dtype) for a in (qg, kgrad, vgrad, wgrad)),
        in_specs=[pl.BlockSpec(memory_space=pltpu.HBM)] * 4,
        compiler_params=pltpu.CompilerParams(vmem_limit_bytes=64 * 2**20),
        out_specs=[pl.BlockSpec(memory_space=pltpu.HBM)] * 4,
        scratch_shapes=[V((SEG, HD), BF16)] * 3 + [V((HD, D), BF16), pltpu.SemaphoreType.DMA((2, 4))],
        name="store_results",
    )(qg, kgrad, vgrad, wgrad)
    return qg[None], kgrad[None], vgrad[None], wgrad


def solution(mesh):
    placed = (
        P("dp", "tm", None),
        P("dp", "tm", None),
        P("dp", "tm", None),
        P("dp", "tm", None),
        P(),
        P("dp", "tm", None),
    )
    return jax.shard_map(
        on_device,
        mesh=mesh,
        in_specs=placed,
        out_specs=(P("dp", "tm", None), P("dp", "tm", None), P("dp", "tm", None), P()),
        check_vma=False,
    )
```

time: 94.4 us -> 80 us (0.85)
  local copies, waits for them, and re-layouts: 8.47 us -> 0 us
  Pallas kernels: 85.1 us -> 79.2 us
    unnamed x16 -> x0, local copies, waits for them, and re-layouts: 8.47 us -> none
    pallas_call x1, Pallas kernels: 85.1 us -> 76.8 us  [on_device(): pl.pallas_call(kernel, out_shape=(jax.ShapeDtypeStruct((SEG, HD), BF16),...]
    pallas_call x0 -> x1, Pallas kernels: none -> 2.47 us  [on_device(): pl.pallas_call(store, out_shape=tuple((jax.ShapeDtypeStruct(a.shape, a.dt...]
where the time goes in v2:
time: 80 us; the launch traced here: 79.9 us
  Pallas kernels  79.2 us (99%)
    pallas_call x1, Pallas kernels, on_device(): pl.pallas_call(kernel, out_shape=(jax.ShapeDtypeStruct((SEG, HD), BF16),...  76.8 us
    pallas_call x1, Pallas kernels, on_device(): pl.pallas_call(store, out_shape=tuple((jax.ShapeDtypeStruct(a.shape, a.dt...  2.47 us

profile of v2, /device:TPU:1, one launch (start us, length us, event | category | flops | bytes accessed | tf_op | source)
XLA Modules:
  0.0 79.9 jit_solution(13552727785967703598)
XLA Ops:
  0.6 76.8 %memory_attention_backward.1 = (bf16[128,512]{1,0:T(8,128)(2,1)}, bf16[128,512]{1,0:T(8,128)(2,1)}, bf16[128,512]{1,0:T(8,128)(2,1)}, bf16[512,1024]{1,0:T(8,128)(2,1)}) custom-call(s32[1,8]{1,0:T(1,128)} %bitcast.12, bf16[128,512]{1,0:T(8,128)(2,1)} %bitcast.9, bf16[128,512]{1,0:T(8,128)(2,1)} %bitcast.10, bf16[128,512]{1,0:T(8,128)(2,1)} %bitcast.11, ...), custom_call_target="tpu_custom_call" | custom-call | tf_op jit(solution)/shard_map/memory_attention_backward/pallas_call | solution.py:608
  77.4 2.5 %store_results.1 = (bf16[128,512]{1,0:T(8,128)(2,1)}, bf16[128,512]{1,0:T(8,128)(2,1)}, bf16[128,512]{1,0:T(8,128)(2,1)}, bf16[512,1024]{1,0:T(8,128)(2,1)}) custom-call(bf16[128,512]{1,0:T(8,128)(2,1)} %get-tuple-element.12.refs_0_, bf16[128,512]{1,0:T(8,128)(2,1)} %get-tuple-element.13.refs_1_, bf16[128,512]{1,0:T(8,128)(2,1)} %get-tuple-element.14.refs_2_, ...), custom_call_target="tpu_custom_call" | custom-call | tf_op jit(solution)/shard_map/store_results/pallas_call | solution.py:624

commit v3 on v2

--- a/solution.py
+++ b/solution.py
@@ -19,11 +19,18 @@
 MESH = pl.DeviceIdType.MESH
 F32, BF16 = jnp.float32, jnp.bfloat16
 
+PARTS = 2
 (
-    C_IDX, C_K, C_V, C_Q, C_G, KZ, KU, KU1, KD, KD1, VY, VU, VU1, VD, VD1,
-    RKY, RKZ, RVZ, RVZ1, RVY, WX, WY, WZ, GY, GC, GD, O_Q, O_K, O_V, GX,
-) = range(30)
-PHASES = GX + NX
+    C_IDX, C_K, C_V, C_Q, C_G, KZ, KU, KD, VY, VU, VD, RKY, RKZ, RVZ, RVZ1, RVY,
+    WX, WY, WZ, GY, GX, GR, GC, GD, O_Q, O_K, O_V,
+) = range(27)
+COUNTS = [(1, 1)] * 27
+COUNTS[KU], COUNTS[KD], COUNTS[VU], COUNTS[VD] = (4 * PARTS,) * 2, (3 * PARTS,) * 2, (1, 4 * PARTS), (1, 3 * PARTS)
+COUNTS[VY] = COUNTS[RKY] = COUNTS[RVY] = (NY, NY)
+COUNTS[GY], COUNTS[GX] = (1, NY), (NX, 7)
+SENDS = [sum(n for n, _ in COUNTS[:i]) for i in range(28)]
+ARRIVALS = [sum(n for _, n in COUNTS[:i]) for i in range(28)]
+FROM_RIGHT, FROM_LEFT, FROM_ACROSS = 0, 5, 6
 
 
 def nt(a, b):
@@ -68,16 +75,26 @@
 
     def remote(src, dst, phase, mine, theirs, device):
         return pltpu.make_async_remote_copy(
-            src_ref=src, dst_ref=dst, send_sem=ssem.at[phase, mine], recv_sem=rsem.at[phase, theirs],
+            src_ref=src, dst_ref=dst, send_sem=ssem.at[SENDS[phase] + mine],
+            recv_sem=rsem.at[ARRIVALS[phase] + theirs],
             device_id=device, device_id_type=MESH,
         )
 
-    def each(count, me, body):
-        def step(d, _):
-            body((me + d) % count)
+    def far(count, k):
+        return count // 2 + (1 - 2 * (k % 2)) * ((k + 1) // 2)
+
+    def arrived(ref, phase, at=0):
+        remote(ref, ref, phase, 0, at, at_core()).wait_recv()
+
+    def left(ref, phase, at=0):
+        remote(ref, ref, phase, at, 0, at_core()).wait_send()
+
+    def each(count, me, body, near=False):
+        def step(k, _):
+            body((me + far(count, count - 2 - k if near else k)) % count)
             return 0
 
-        lax.fori_loop(1, count, step, 0)
+        lax.fori_loop(0, count - 1, step, 0)
 
     def span(lo, hi, body):
         def step(i, _):
@@ -157,8 +174,8 @@
     kbuf[y, blk(z)] = nn(oh[...], k_pair).astype(BF16)
     vbuf[y, blk(z)] = nn(oh[...], v_pair).astype(BF16)
 
-    each(NZ, z, lambda i: remote(kbuf.at[y, blk(z)], kbuf.at[y, blk(z)], KZ, i, z, at_z(i)).start())
-    span(y + 1, NY, lambda i: remote(vbuf.at[y, blk(z)], vbuf.at[y, blk(z)], VY, i, y, at_y(i)).start())
+    each(NZ, z, lambda i: remote(kbuf.at[y, blk(z)], kbuf.at[y, blk(z)], KZ, 0, 0, at_z(i)).start())
+    span(0, NY - 1 - y, lambda i: remote(vbuf.at[y, blk(z)], vbuf.at[y, blk(z)], VY, NY - 1 - i, y, at_y(NY - 1 - i)).start())
 
     local[3].wait()
     swaps[3].wait_recv()
@@ -186,41 +203,42 @@
     for h in range(HEADS):
         ga4[pl.ds(h * 256, 256), :] = jnp.where(lanes == h, ga, jnp.zeros_like(ga))
 
-    each(NZ, z, lambda i: remote(kbuf.at[y, blk(z)], kbuf.at[y, blk(i)], KZ, i, i, at_z(i)).wait_recv())
+    arrived(kbuf.at[y, pl.ds(0, 112)], KZ)
 
     up_y, dn_y, up_z, dn_z = (y + 1) % NY, (y + NY - 1) % NY, (z + 1) % NZ, (z + NZ - 1) % NZ
 
-    def k_pass(phase, device, b, part):
-        ref = kbuf.at[b, pl.ds(part * 64, 64)]
-        return remote(ref, ref, phase + part, b, b, device)
-
-    def v_pass(phase, device, b, part):
-        ref = vbuf.at[pl.ds(part * 4, 4), blk(b)]
-        return remote(ref, ref, phase + part, b, b, device)
-
-    def k_up(b, part):
-        return k_pass(KU, at_y(up_y), b, part)
-
-    def k_dn(b, part):
-        return k_pass(KD, at_y(dn_y), b, part)
-
-    def v_up(b, part):
-        return v_pass(VU, at_z(up_z), b, part)
-
-    def v_dn(b, part):
-        return v_pass(VD, at_z(dn_z), b, part)
+    def k_pass(phase, device, b, part, hops):
+        ref = kbuf.at[b, pl.ds(part * (SEG // PARTS), SEG // PARTS)]
+        at = hops * PARTS + part
+        return remote(ref, ref, phase, at, at, device)
+
+    def v_pass(phase, device, b, part, hops):
+        ref = vbuf.at[pl.ds(part * (NY // PARTS), NY // PARTS), blk(b)]
+        return remote(ref, ref, phase, 0, hops * PARTS + part, device)
+
+    def k_up(b, part, hops):
+        return k_pass(KU, at_y(up_y), b, part, hops)
+
+    def k_dn(b, part, hops):
+        return k_pass(KD, at_y(dn_y), b, part, hops)
+
+    def v_up(b, part, hops):
+        return v_pass(VU, at_z(up_z), b, part, hops)
+
+    def v_dn(b, part, hops):
+        return v_pass(VD, at_z(dn_z), b, part, hops)
 
     def begin(copy, b):
-        copy(b, 0).start()
-        copy(b, 1).start()
-
-    def hand_on(copy, b, more):
-        for part in range(2):
-            copy(b, part).wait_recv()
+        for part in range(PARTS):
+            copy(b, part, 0).start()
+
+    def hand_on(copy, b, step, more):
+        for part in range(PARTS):
+            copy(b, part, step - 1).wait_recv()
 
             @pl.when(more)
             def _():
-                copy(b, part).start()
+                copy(b, part, step).start()
 
     @pl.when(y < NY - 1)
     def _():
@@ -254,17 +272,16 @@
 
         @pl.when(below >= 0)
         def _():
-            hand_on(k_up, below, (step < 4) & (y < NY - 1))
+            hand_on(k_up, below, step, (step < 4) & (y < NY - 1))
 
         @pl.when(from_above)
         def _():
-            hand_on(k_dn, above, step < 3)
-
-        hand_on(v_up, (z + NZ - step) % NZ, step < 4)
+            hand_on(k_dn, above, step, step < 3)
 
         @pl.when(step <= 3)
         def _():
-            hand_on(v_dn, (z + step) % NZ, step < 3)
+            hand_on(v_up, (z + NZ - step) % NZ, step, step < 4)
+            hand_on(v_dn, (z + step) % NZ, step, step < 3)
 
         @pl.when(below >= 0)
         def _():
@@ -305,9 +322,16 @@
         p = jnp.exp(s_mem[two(i)].reshape(2 * SEG, COLS) - top)
         s_mem[two(i)] = p.reshape(2, SEG, COLS)
         l8[...] = l8[...] + rows8(p, jnp.sum)
-        add_attended(vbuf[two(i)].reshape(2 * SEG, HALF), p)
 
     span(0, pairs, soft_of)
+
+    for part in range(PARTS):
+        v_up((z + NZ - 4) % NZ, part, 3).wait_recv()
+
+    def attended_of(i):
+        add_attended(vbuf[two(i)].reshape(2 * SEG, HALF), s_mem[two(i)].reshape(2 * SEG, COLS))
+
+    span(0, pairs, attended_of)
     inv = 1.0 / jnp.sum(l8[...], axis=0, keepdims=True)
     att = jnp.concatenate(
         [acc[h * HEAD_DIM : (h + 1) * HEAD_DIM, :] * inv[:, h * 256 : (h + 1) * 256] for h in range(HEADS)], 0
@@ -319,7 +343,7 @@
     def wrows(i):
         return pl.ds(pl.multiple_of(i * 64, 64), 64)
 
-    each(NX, dp, lambda i: remote(wsend.at[wrows(i)], wxr.at[dp], WX, i, dp, at_x(i)).start())
+    each(NX, dp, lambda i: remote(wsend.at[wrows(i)], wxr.at[dp], WX, 0, 0, at_x(i)).start())
 
     prod = att.astype(F32) * gat[...]
     delta = jnp.concatenate(
@@ -360,7 +384,7 @@
 
     def v_send(half, i):
         part = pl.ds(half * 4, 4)
-        return remote(vt.at[part, blk(i)], vrz.at[z, part], RVZ + half, i, z, at_z(i))
+        return remote(vt.at[part, blk(i)], vrz.at[z, part], RVZ + half, 0, 0, at_z(i))
 
     def v_half(half):
         each(NZ, z, lambda i: v_send(half, i).start())
@@ -385,28 +409,54 @@
     keep_q = pltpu.make_async_copy(obq.at[c], qo_ref.at[:, my_cols], lsem.at[6])
     keep_q.start()
 
+    for s in swaps:
+        s.wait_send()
+    left(kbuf.at[y, pl.ds(0, 112)], KZ)
+    span(y + 1, NY, lambda i: remote(vbuf.at[y, blk(z)], vbuf.at[y, blk(z)], VY, i, y, at_y(i)).wait_send())
+
+    def sent(copy, b, step):
+        for part in range(PARTS):
+            copy(b, part, step).wait_send()
+
+    def gather_sent(step):
+        below, above = y - step, (y + step) % NY
+
+        @pl.when((below >= 0) & (y < NY - 1))
+        def _():
+            sent(k_up, below, step)
+
+        @pl.when((step < 3) & (above <= 2))
+        def _():
+            sent(k_dn, above, step)
+
+    span(0, 4, gather_sent)
+    left(vbuf.at[:, pl.ds(0, 64)], VU)
+    left(vbuf.at[:, pl.ds(0, 48)], VD)
+
+    arrived(wxr.at[pl.ds(0, NX - 1)], WX)
+
     def add_x(i):
-        remote(wsend.at[wrows(i)], wxr.at[i], WX, i, i, at_x(i)).wait_recv()
         wt[wrows(dp), :] = wt[wrows(dp), :] + wxr[i].astype(F32)
 
-    each(NX, dp, add_x)
+    each(NX, dp, add_x, near=True)
     wxs[...] = wt[wrows(dp), :].astype(BF16)
 
     def wcols(i):
         return pl.ds(pl.multiple_of(i * 128, 128), 128)
 
-    each(NY, y, lambda i: remote(wxs.at[:, wcols(i)], wyr.at[y], WY, i, y, at_y(i)).start())
+    each(NY, y, lambda i: remote(wxs.at[:, wcols(i)], wyr.at[y], WY, 0, 0, at_y(i)).start())
+    left(wsend.at[pl.ds(0, 192)], WX)
 
     def add_vz(half):
         part = pl.ds(half * 4, 4)
+        arrived(vrz.at[pl.ds(0, NZ - 1), part], RVZ + half)
+        left(vt.at[part, pl.ds(0, 112)], RVZ + half)
         vsum[part] = vt[part, blk(z)].astype(F32)
 
         def add(i):
-            v_send(half, i).wait_send()
-            remote(vt.at[part, blk(i)], vrz.at[i, part], RVZ + half, i, i, at_z(i)).wait_recv()
             vsum[part] = vsum[part] + vrz[i, part].astype(F32)
 
-        each(NZ, z, add)
+        each(NZ, z, add, near=True)
 
     add_vz(0)
 
@@ -419,13 +469,16 @@
 
     wys[...] = wt[wrows(dp), wcols(y)]
 
+    arrived(wyr.at[pl.ds(0, NY - 1)], WY)
+
     def add_y(i):
-        remote(wxs.at[:, wcols(i)], wyr.at[i], WY, i, i, at_y(i)).wait_recv()
         wys[...] = wys[...] + wyr[i].astype(F32)
 
-    each(NY, y, add_y)
+    each(NY, y, add_y, near=True)
     wzr[z] = wys[...].astype(BF16)
-    each(NZ, z, lambda i: remote(wzr.at[z], wzr.at[z], WZ, i, z, at_z(i)).start())
+    each(NZ, z, lambda i: remote(wzr.at[z], wzr.at[z], WZ, 0, 0, at_z(i)).start())
+    left(wxs.at[:, pl.ds(0, 896)], WY)
+    span(0, y, lambda i: remote(kt.at[i], kry.at[y], RKY, i, y, at_y(i)).wait_send())
 
     ksum[...] = kt[y].astype(F32)
 
@@ -435,9 +488,9 @@
 
     span(y + 1, NY, add_ky)
     krow[...] = ksum[...].astype(BF16)
-    each(NZ, z, lambda i: remote(krow.at[blk(i)], krz.at[z], RKZ, i, z, at_z(i)).start())
-
-    each(NZ, z, lambda i: remote(wzr.at[z], wzr.at[i], WZ, i, i, at_z(i)).wait_recv())
+    each(NZ, z, lambda i: remote(krow.at[blk(i)], krz.at[z], RKZ, 0, 0, at_z(i)).start())
+
+    arrived(wzr.at[pl.ds(0, NZ - 1)], WZ)
     total = wzr[0].astype(F32)
     for i in range(1, NZ):
         total = total + wzr[i].astype(F32)
@@ -454,27 +507,49 @@
     wo_ref[wrows(dp), wcols(y)] = (total * (1.0 / math.sqrt(4 * 16384))).astype(BF16)
     here = piece(dp, y)
 
-    def send_x(i, j):
-        return pltpu.make_async_remote_copy(
-            src_ref=piece(dp, j), dst_ref=piece(dp, j), send_sem=ssem.at[GX + i, j], recv_sem=rsem.at[GX + dp, j],
-            device_id=at_x(i), device_id_type=MESH,
-        )
-
-    def to_x(j):
-        each(NX, dp, lambda i: send_x(i, j).start())
-        remote(piece(dp, j), out_piece(c, dp, j), GC, j, j, at_core()).start()
+    def send_x(i, j, at):
+        return remote(piece(dp, j), piece(dp, j), GX, i, at, at_x(i))
+
+    x_up, x_dn, across = (dp + 1) % NX, (dp + 3) % NX, (dp + 2) % NX
+
+    def nth(n):
+        return (y + (1 - 2 * (n % 2)) * ((n + 1) // 2)) % NY
+
+    def to_x(n):
+        j = nth(n)
+        send_x(x_up, j, FROM_LEFT).start()
+        send_x(x_dn, j, FROM_RIGHT + n - n // 4 * (n - 4)).start()
+
+        @pl.when(n >= 4)
+        def _():
+            send_x(across, j, FROM_ACROSS).start()
+
+        remote(piece(dp, j), out_piece(c, dp, j), GC, 0, 0, at_core()).start()
+
+    mine = wo_ref.at[wrows(dp)]
 
     def keep(i):
-        return pltpu.make_async_copy(wo_ref.at[wrows(i)], out_rows(c, i), lsem.at[9 + i])
-
-    each(NY, y, lambda i: remote(here, here, GY, i, y, at_y(i)).start())
-    to_x(y)
-
-    def from_y(i):
+        return pltpu.make_async_copy(wo_ref.at[wrows(i)], out_rows(c, i), lsem.at[9])
+
+    each(NY, y, lambda i: remote(here, here, GY, 0, y, at_y(i)).start())
+    to_x(0)
+
+    def from_y(n):
+        i = nth(n)
         remote(here, piece(dp, i), GY, i, i, at_y(i)).wait_recv()
-        to_x(i)
-
-    each(NY, y, from_y)
+        to_x(n)
+
+    span(1, NY, from_y)
+
+    def pass_on(n):
+        ref = piece(x_up, nth(n))
+        arrived(ref, GX, FROM_RIGHT + n)
+        pltpu.make_async_remote_copy(
+            src_ref=ref, dst_ref=ref, send_sem=ssem.at[SENDS[GR]], recv_sem=rsem.at[ARRIVALS[GX] + FROM_ACROSS],
+            device_id=at_x(x_dn), device_id_type=MESH,
+        ).start()
+
+    span(0, 4, pass_on)
     keep(dp).start()
 
     vsum_own[...] = vsum[y]
@@ -486,11 +561,12 @@
     span(y + 1, NY, add_vy)
     kown = ksum.at[blk(z)]
 
+    arrived(krz.at[pl.ds(0, NZ - 1)], RKZ)
+
     def add_kz(i):
-        remote(krow.at[blk(i)], krz.at[i], RKZ, i, i, at_z(i)).wait_recv()
         kown[...] = kown[...] + krz[i].astype(F32)
 
-    each(NZ, z, add_kz)
+    each(NZ, z, add_kz, near=True)
 
     def place(local, terms):
         hi = terms.astype(BF16)
@@ -508,63 +584,35 @@
     keep_k.start()
     keep_v.start()
 
-    def from_x(i):
-        span(0, NY, lambda j: remote(piece(i, j), piece(i, j), GX + i, j, j, at_x(i)).wait_recv())
-        remote(wo_ref.at[wrows(i)], out_rows(c, i), GD, i, i, at_core()).start()
+    left(krow.at[pl.ds(0, 112)], RKZ)
+    span(0, y, lambda i: remote(vrow.at[i], vry.at[y], RVY, i, y, at_y(i)).wait_send())
+    left(wzr.at[pl.ds(0, NZ - 1)], WZ)
+    out_q.wait()
+    out_k.wait()
+    out_v.wait()
+
+    def from_x(i, first, at):
+        arrived(wo_ref.at[wrows(i), pl.ds(0, (NY - first) * 128)], GX, at)
+        remote(wo_ref.at[wrows(i)], out_rows(c, i), GD, 0, 0, at_core()).start()
         keep(i).start()
 
-    each(NX, dp, from_x)
-    span(0, NY, lambda j: remote(here, out_piece(other, dp, j), GC, j, j, at_core()).wait_recv())
-    each(NX, dp, lambda i: remote(wo_ref.at[wrows(i)], out_rows(other, i), GD, i, i, at_core()).wait_recv())
-    span(0, NX, lambda i: keep(i).wait())
+    from_x(x_up, 4, FROM_RIGHT + 4)
+    from_x(x_dn, 0, FROM_LEFT)
+    from_x(across, 0, FROM_ACROSS)
+    arrived(out_rows(other, dp), GC)
+    arrived(wout_ref.at[pl.ds(0, 192)], GD)
+    pltpu.make_async_copy(wo_ref, wout_ref.at[pl.ds(0, HALF)], lsem.at[9]).wait()
     keep_q.wait()
     keep_k.wait()
     keep_v.wait()
 
-    out_q.wait()
-    out_k.wait()
-    out_v.wait()
-    for s in swaps:
-        s.wait_send()
-    each(NZ, z, lambda i: remote(kbuf.at[y, blk(z)], kbuf.at[y, blk(z)], KZ, i, z, at_z(i)).wait_send())
-    span(y + 1, NY, lambda i: remote(vbuf.at[y, blk(z)], vbuf.at[y, blk(z)], VY, i, y, at_y(i)).wait_send())
-
-    def sent(copy, b):
-        copy(b, 0).wait_send()
-        copy(b, 1).wait_send()
-
-    def gather_sent(step):
-        below, above = y - step, (y + step) % NY
-
-        @pl.when((below >= 0) & (step < 4) & (y < NY - 1))
-        def _():
-            sent(k_up, below)
-
-        @pl.when((step < 3) & (above <= 2))
-        def _():
-            sent(k_dn, above)
-
-        sent(v_up, (z + NZ - step) % NZ)
-
-        @pl.when(step < 3)
-        def _():
-            sent(v_dn, (z + step) % NZ)
-
-    span(0, 4, gather_sent)
-    each(NX, dp, lambda i: remote(wsend.at[wrows(i)], wxr.at[dp], WX, i, dp, at_x(i)).wait_send())
-    span(0, y, lambda i: remote(kt.at[i], kry.at[y], RKY, i, y, at_y(i)).wait_send())
-    each(NY, y, lambda i: remote(wxs.at[:, wcols(i)], wyr.at[y], WY, i, y, at_y(i)).wait_send())
-    each(NZ, z, lambda i: remote(krow.at[blk(i)], krz.at[z], RKZ, i, z, at_z(i)).wait_send())
-    span(0, y, lambda i: remote(vrow.at[i], vry.at[y], RVY, i, y, at_y(i)).wait_send())
-    each(NZ, z, lambda i: remote(wzr.at[z], wzr.at[z], WZ, i, z, at_z(i)).wait_send())
-    each(NY, y, lambda i: remote(here, here, GY, i, y, at_y(i)).wait_send())
-    span(0, NY, lambda j: remote(piece(dp, j), out_piece(c, dp, j), GC, j, j, at_core()).wait_send())
-
-    def x_sent(i):
-        span(0, NY, lambda j: send_x(i, j).wait_send())
-        remote(wo_ref.at[wrows(i)], out_rows(c, i), GD, i, i, at_core()).wait_send()
-
-    each(NX, dp, x_sent)
+    left(wo_ref.at[pl.ds(0, 64), pl.ds(0, 896)], GY)
+    left(mine, GC)
+    left(mine, GX, x_up)
+    left(mine, GX, x_dn)
+    left(wo_ref.at[wrows(dp), pl.ds(0, D // 2)], GX, across)
+    left(wo_ref.at[pl.ds(0, 64), pl.ds(0, D // 2)], GR)
+    left(wo_ref.at[pl.ds(0, 192)], GD)
 
 
 def store(*refs):
@@ -603,7 +651,7 @@
         V((NY, 64, 128), BF16), V((64, 128), F32),
         V((NZ, 64, 128), BF16), V((HALF, D), BF16),
         V((2, SEG, HALF), BF16), V((2, SEG, HALF), BF16), V((2, SEG, HALF), BF16),
-        pltpu.SemaphoreType.DMA((PHASES, 8)), pltpu.SemaphoreType.DMA((PHASES, 8)), pltpu.SemaphoreType.DMA((9 + NX,)),
+        pltpu.SemaphoreType.DMA((SENDS[-1],)), pltpu.SemaphoreType.DMA((ARRIVALS[-1],)), pltpu.SemaphoreType.DMA((10,)),
     ]
     qg, kgrad, vgrad, wgrad = pl.pallas_call(
         kernel,

time: 80 us -> 73.7 us (0.921)
  Pallas kernels: 79.2 us -> 72.9 us
    pallas_call x1, Pallas kernels: 76.8 us -> 70.4 us  [on_device(): pl.pallas_call(kernel, out_shape=(jax.ShapeDtypeStruct((SEG, HD), BF16),...]
where the time goes in v3:
time: 73.7 us; the launch traced here: 73.5 us
  Pallas kernels  72.9 us (99%)
    pallas_call x1, Pallas kernels, on_device(): pl.pallas_call(kernel, out_shape=(jax.ShapeDtypeStruct((SEG, HD), BF16),...  70.4 us
    pallas_call x1, Pallas kernels, on_device(): pl.pallas_call(store, out_shape=tuple((jax.ShapeDtypeStruct(a.shape, a.dt...  2.47 us

profile of v3, /device:TPU:1, one launch (start us, length us, event | category | flops | bytes accessed | tf_op | source)
XLA Modules:
  0.0 73.5 jit_solution(540738805139496032)
XLA Ops:
  0.6 70.4 %memory_attention_backward.1 = (bf16[128,512]{1,0:T(8,128)(2,1)}, bf16[128,512]{1,0:T(8,128)(2,1)}, bf16[128,512]{1,0:T(8,128)(2,1)}, bf16[512,1024]{1,0:T(8,128)(2,1)}) custom-call(s32[1,8]{1,0:T(1,128)} %bitcast.12, bf16[128,512]{1,0:T(8,128)(2,1)} %bitcast.9, bf16[128,512]{1,0:T(8,128)(2,1)} %bitcast.10, bf16[128,512]{1,0:T(8,128)(2,1)} %bitcast.11, ...), custom_call_target="tpu_custom_call" | custom-call | tf_op jit(solution)/shard_map/memory_attention_backward/pallas_call | solution.py:656
  71.1 2.5 %store_results.1 = (bf16[128,512]{1,0:T(8,128)(2,1)}, bf16[128,512]{1,0:T(8,128)(2,1)}, bf16[128,512]{1,0:T(8,128)(2,1)}, bf16[512,1024]{1,0:T(8,128)(2,1)}) custom-call(bf16[128,512]{1,0:T(8,128)(2,1)} %get-tuple-element.12.refs_0_, bf16[128,512]{1,0:T(8,128)(2,1)} %get-tuple-element.13.refs_1_, bf16[128,512]{1,0:T(8,128)(2,1)} %get-tuple-element.14.refs_2_, ...), custom_call_target="tpu_custom_call" | custom-call | tf_op jit(solution)/shard_map/store_results/pallas_call | solution.py:672

commit v4 on v3

--- a/solution.py
+++ b/solution.py
@@ -447,6 +447,29 @@
     each(NY, y, lambda i: remote(wxs.at[:, wcols(i)], wyr.at[y], WY, 0, 0, at_y(i)).start())
     left(wsend.at[pl.ds(0, 192)], WX)
 
+    wys[...] = wt[wrows(dp), wcols(y)]
+
+    arrived(wyr.at[pl.ds(0, NY - 1)], WY)
+
+    def add_y(i):
+        wys[...] = wys[...] + wyr[i].astype(F32)
+
+    each(NY, y, add_y, near=True)
+    wzr[z] = wys[...].astype(BF16)
+    each(NZ, z, lambda i: remote(wzr.at[z], wzr.at[z], WZ, 0, 0, at_z(i)).start())
+    left(wxs.at[:, pl.ds(0, 896)], WY)
+    span(0, y, lambda i: remote(kt.at[i], kry.at[y], RKY, i, y, at_y(i)).wait_send())
+
+    ksum[...] = kt[y].astype(F32)
+
+    def add_ky(i):
+        remote(kt.at[0], kry.at[i], RKY, 0, i, at_y(i)).wait_recv()
+        ksum[...] = ksum[...] + kry[i].astype(F32)
+
+    span(y + 1, NY, add_ky)
+    krow[...] = ksum[...].astype(BF16)
+    each(NZ, z, lambda i: remote(krow.at[blk(i)], krz.at[z], RKZ, 0, 0, at_z(i)).start())
+
     def add_vz(half):
         part = pl.ds(half * 4, 4)
         arrived(vrz.at[pl.ds(0, NZ - 1), part], RVZ + half)
@@ -467,29 +490,6 @@
     vrow[...] = vsum[...].astype(BF16)
     span(0, y, lambda i: remote(vrow.at[i], vry.at[y], RVY, i, y, at_y(i)).start())
 
-    wys[...] = wt[wrows(dp), wcols(y)]
-
-    arrived(wyr.at[pl.ds(0, NY - 1)], WY)
-
-    def add_y(i):
-        wys[...] = wys[...] + wyr[i].astype(F32)
-
-    each(NY, y, add_y, near=True)
-    wzr[z] = wys[...].astype(BF16)
-    each(NZ, z, lambda i: remote(wzr.at[z], wzr.at[z], WZ, 0, 0, at_z(i)).start())
-    left(wxs.at[:, pl.ds(0, 896)], WY)
-    span(0, y, lambda i: remote(kt.at[i], kry.at[y], RKY, i, y, at_y(i)).wait_send())
-
-    ksum[...] = kt[y].astype(F32)
-
-    def add_ky(i):
-        remote(kt.at[0], kry.at[i], RKY, 0, i, at_y(i)).wait_recv()
-        ksum[...] = ksum[...] + kry[i].astype(F32)
-
-    span(y + 1, NY, add_ky)
-    krow[...] = ksum[...].astype(BF16)
-    each(NZ, z, lambda i: remote(krow.at[blk(i)], krz.at[z], RKZ, 0, 0, at_z(i)).start())
-
     arrived(wzr.at[pl.ds(0, NZ - 1)], WZ)
     total = wzr[0].astype(F32)
     for i in range(1, NZ):
@@ -533,24 +533,6 @@
 
     each(NY, y, lambda i: remote(here, here, GY, 0, y, at_y(i)).start())
     to_x(0)
-
-    def from_y(n):
-        i = nth(n)
-        remote(here, piece(dp, i), GY, i, i, at_y(i)).wait_recv()
-        to_x(n)
-
-    span(1, NY, from_y)
-
-    def pass_on(n):
-        ref = piece(x_up, nth(n))
-        arrived(ref, GX, FROM_RIGHT + n)
-        pltpu.make_async_remote_copy(
-            src_ref=ref, dst_ref=ref, send_sem=ssem.at[SENDS[GR]], recv_sem=rsem.at[ARRIVALS[GX] + FROM_ACROSS],
-            device_id=at_x(x_dn), device_id_type=MESH,
-        ).start()
-
-    span(0, 4, pass_on)
-    keep(dp).start()
 
     vsum_own[...] = vsum[y]
 
@@ -584,12 +566,27 @@
     keep_k.start()
     keep_v.start()
 
+    def from_y(n):
+        i = nth(n)
+        remote(here, piece(dp, i), GY, i, i, at_y(i)).wait_recv()
+        to_x(n)
+
+    span(1, NY, from_y)
+
+    def pass_on(n):
+        ref = piece(x_up, nth(n))
+        arrived(ref, GX, FROM_RIGHT + n)
+        pltpu.make_async_remote_copy(
+            src_ref=ref, dst_ref=ref, send_sem=ssem.at[SENDS[GR]], recv_sem=rsem.at[ARRIVALS[GX] + FROM_ACROSS],
+            device_id=at_x(x_dn), device_id_type=MESH,
+        ).start()
+
+    span(0, 4, pass_on)
+    keep(dp).start()
+
     left(krow.at[pl.ds(0, 112)], RKZ)
     span(0, y, lambda i: remote(vrow.at[i], vry.at[y], RVY, i, y, at_y(i)).wait_send())
     left(wzr.at[pl.ds(0, NZ - 1)], WZ)
-    out_q.wait()
-    out_k.wait()
-    out_v.wait()
 
     def from_x(i, first, at):
         arrived(wo_ref.at[wrows(i), pl.ds(0, (NY - first) * 128)], GX, at)
@@ -606,6 +603,9 @@
     keep_k.wait()
     keep_v.wait()
 
+    out_q.wait()
+    out_k.wait()
+    out_v.wait()
     left(wo_ref.at[pl.ds(0, 64), pl.ds(0, 896)], GY)
     left(mine, GC)
     left(mine, GX, x_up)
@@ -617,8 +617,15 @@
 
 def store(*refs):
     arrays, outs, held, sem = refs[:4], refs[4:8], refs[8:12], refs[12]
-    loads = [pltpu.make_async_copy(arrays[i], held[i], sem.at[0, i]) for i in range(4)]
-    stores = [pltpu.make_async_copy(held[i], outs[i], sem.at[1, i]) for i in range(4)]
+    parts = [(3, 128 * i) for i in range(4)] + [(0, 0), (1, 0), (2, 0)]
+
+    def moves(source, target, row):
+        return [
+            pltpu.make_async_copy(source[a].at[pl.ds(r, SEG)], target[a].at[pl.ds(r, SEG)], sem.at[row, i])
+            for i, (a, r) in enumerate(parts)
+        ]
+
+    loads, stores = moves(arrays, held, 0), moves(held, outs, 1)
     for copy in loads:
         copy.start()
     for load, copy in zip(loads, stores):
@@ -675,7 +682,7 @@
         in_specs=[pl.BlockSpec(memory_space=pltpu.HBM)] * 4,
         compiler_params=pltpu.CompilerParams(vmem_limit_bytes=64 * 2**20),
         out_specs=[pl.BlockSpec(memory_space=pltpu.HBM)] * 4,
-        scratch_shapes=[V((SEG, HD), BF16)] * 3 + [V((HD, D), BF16), pltpu.SemaphoreType.DMA((2, 4))],
+        scratch_shapes=[V((SEG, HD), BF16)] * 3 + [V((HD, D), BF16), pltpu.SemaphoreType.DMA((2, 7))],
         name="store_results",
     )(qg, kgrad, vgrad, wgrad)
     return qg[None], kgrad[None], vgrad[None], wgrad

time: 73.7 us -> 72.8 us (0.988)
  Pallas kernels: 72.9 us -> 72 us
where the time goes in v4:
time: 72.8 us; the launch traced here: 72.7 us
  Pallas kernels  72 us (99%)
    pallas_call x1, Pallas kernels, on_device(): pl.pallas_call(kernel, out_shape=(jax.ShapeDtypeStruct((SEG, HD), BF16),...  69.9 us
    pallas_call x1, Pallas kernels, on_device(): pl.pallas_call(store, out_shape=tuple((jax.ShapeDtypeStruct(a.shape, a.dt...  2.16 us

profile of v4, /device:TPU:1, one launch (start us, length us, event | category | flops | bytes accessed | tf_op | source)
XLA Modules:
  0.0 72.7 jit_solution(1689632669633483769)
XLA Ops:
  0.6 69.9 %memory_attention_backward.1 = (bf16[128,512]{1,0:T(8,128)(2,1)}, bf16[128,512]{1,0:T(8,128)(2,1)}, bf16[128,512]{1,0:T(8,128)(2,1)}, bf16[512,1024]{1,0:T(8,128)(2,1)}) custom-call(s32[1,8]{1,0:T(1,128)} %bitcast.12, bf16[128,512]{1,0:T(8,128)(2,1)} %bitcast.9, bf16[128,512]{1,0:T(8,128)(2,1)} %bitcast.10, bf16[128,512]{1,0:T(8,128)(2,1)} %bitcast.11, ...), custom_call_target="tpu_custom_call" | custom-call | tf_op jit(solution)/shard_map/memory_attention_backward/pallas_call | solution.py:663
  70.5 2.2 %store_results.1 = (bf16[128,512]{1,0:T(8,128)(2,1)}, bf16[128,512]{1,0:T(8,128)(2,1)}, bf16[128,512]{1,0:T(8,128)(2,1)}, bf16[512,1024]{1,0:T(8,128)(2,1)}) custom-call(bf16[128,512]{1,0:T(8,128)(2,1)} %get-tuple-element.12.refs_0_, bf16[128,512]{1,0:T(8,128)(2,1)} %get-tuple-element.13.refs_1_, bf16[128,512]{1,0:T(8,128)(2,1)} %get-tuple-element.14.refs_2_, ...), custom_call_target="tpu_custom_call" | custom-call | tf_op jit(solution)/shard_map/store_results/pallas_call | solution.py:679

commit v5 on v4

--- a/solution.py
+++ b/solution.py
@@ -26,10 +26,12 @@
 ) = range(27)
 COUNTS = [(1, 1)] * 27
 COUNTS[KU], COUNTS[KD], COUNTS[VU], COUNTS[VD] = (4 * PARTS,) * 2, (3 * PARTS,) * 2, (1, 4 * PARTS), (1, 3 * PARTS)
-COUNTS[VY] = COUNTS[RKY] = COUNTS[RVY] = (NY, NY)
+COUNTS[VY] = COUNTS[RKY] = (NY, NY)
+COUNTS[RVY] = (0, 0)
 COUNTS[GY], COUNTS[GX] = (1, NY), (NX, 7)
 SENDS = [sum(n for n, _ in COUNTS[:i]) for i in range(28)]
 ARRIVALS = [sum(n for _, n in COUNTS[:i]) for i in range(28)]
+SENDS[RVY], ARRIVALS[RVY] = SENDS[VY], ARRIVALS[VY]
 FROM_RIGHT, FROM_LEFT, FROM_ACROSS = 0, 5, 6
 
 
@@ -111,6 +113,16 @@
 
     kbuf[...] = jnp.zeros_like(kbuf)
     vbuf[...] = jnp.zeros_like(vbuf)
+
+    bar = pltpu.get_barrier_semaphore()
+
+    def greet(device):
+        pl.semaphore_signal(bar, inc=1, device_id=device, device_id_type=MESH)
+
+    greet(at_core())
+    each(NZ, z, lambda i: greet(at_z(i)))
+    each(NY, y, lambda i: greet(at_y(i)))
+    each(NX, dp, lambda i: greet(at_x(i)))
 
     local = [
         pltpu.make_async_copy(src, dst, lsem.at[i])
@@ -125,16 +137,6 @@
     ]
     for copy in local:
         copy.start()
-
-    bar = pltpu.get_barrier_semaphore()
-
-    def greet(device):
-        pl.semaphore_signal(bar, inc=1, device_id=device, device_id_type=MESH)
-
-    greet(at_core())
-    each(NZ, z, lambda i: greet(at_z(i)))
-    each(NY, y, lambda i: greet(at_y(i)))
-    each(NX, dp, lambda i: greet(at_x(i)))
 
     vt[...] = jnp.zeros_like(vt)
     pl.semaphore_wait(bar, 1 + (NZ - 1) + (NY - 1) + (NX - 1))
@@ -158,8 +160,7 @@
     swaps[3].start()
     swaps[4].start()
     local[1].wait()
-    local[2].wait()
-    for s in swaps[:3]:
+    for s in swaps[:2]:
         s.wait_recv()
 
     lane = lax.broadcasted_iota(jnp.int32, (MEM, SEG), 1)
@@ -170,11 +171,13 @@
         [jnp.concatenate([one_a, zero], 1), jnp.concatenate([zero, one_b], 1)], 0
     ).astype(BF16)
     k_pair = kp[...].reshape(2 * SEG, HALF)
+    kbuf[y, blk(z)] = nn(oh[...], k_pair).astype(BF16)
+
+    each(NZ, z, lambda i: remote(kbuf.at[y, blk(z)], kbuf.at[y, blk(z)], KZ, 0, 0, at_z(i)).start())
+    local[2].wait()
+    swaps[2].wait_recv()
     v_pair = vp[...].reshape(2 * SEG, HALF)
-    kbuf[y, blk(z)] = nn(oh[...], k_pair).astype(BF16)
     vbuf[y, blk(z)] = nn(oh[...], v_pair).astype(BF16)
-
-    each(NZ, z, lambda i: remote(kbuf.at[y, blk(z)], kbuf.at[y, blk(z)], KZ, 0, 0, at_z(i)).start())
     span(0, NY - 1 - y, lambda i: remote(vbuf.at[y, blk(z)], vbuf.at[y, blk(z)], VY, NY - 1 - i, y, at_y(NY - 1 - i)).start())
 
     local[3].wait()

time: 72.8 us -> 72.5 us (level)
  no operation moved by 1% of the time
where the time goes in v5:
time: 72.5 us; the launch traced here: 72.3 us
  Pallas kernels  71.7 us (99%)
    pallas_call x1, Pallas kernels, on_device(): pl.pallas_call(kernel, out_shape=(jax.ShapeDtypeStruct((SEG, HD), BF16),...  69.5 us
    pallas_call x1, Pallas kernels, on_device(): pl.pallas_call(store, out_shape=tuple((jax.ShapeDtypeStruct(a.shape, a.dt...  2.16 us

profile of v5, /device:TPU:1, one launch (start us, length us, event | category | flops | bytes accessed | tf_op | source)
XLA Modules:
  0.0 72.3 jit_solution(6196698055102608287)
XLA Ops:
  0.6 69.5 %memory_attention_backward.1 = (bf16[128,512]{1,0:T(8,128)(2,1)}, bf16[128,512]{1,0:T(8,128)(2,1)}, bf16[128,512]{1,0:T(8,128)(2,1)}, bf16[512,1024]{1,0:T(8,128)(2,1)}) custom-call(s32[1,8]{1,0:T(1,128)} %bitcast.12, bf16[128,512]{1,0:T(8,128)(2,1)} %bitcast.9, bf16[128,512]{1,0:T(8,128)(2,1)} %bitcast.10, bf16[128,512]{1,0:T(8,128)(2,1)} %bitcast.11, ...), custom_call_target="tpu_custom_call" | custom-call | tf_op jit(solution)/shard_map/memory_attention_backward/pallas_call | solution.py:666
  70.2 2.2 %store_results.1 = (bf16[128,512]{1,0:T(8,128)(2,1)}, bf16[128,512]{1,0:T(8,128)(2,1)}, bf16[128,512]{1,0:T(8,128)(2,1)}, bf16[512,1024]{1,0:T(8,128)(2,1)}) custom-call(bf16[128,512]{1,0:T(8,128)(2,1)} %get-tuple-element.12.refs_0_, bf16[128,512]{1,0:T(8,128)(2,1)} %get-tuple-element.13.refs_1_, bf16[128,512]{1,0:T(8,128)(2,1)} %get-tuple-element.14.refs_2_, ...), custom_call_target="tpu_custom_call" | custom-call | tf_op jit(solution)/shard_map/store_results/pallas_call | solution.py:682
